TPU v7x, 128 devices: a whole 4x4x4 slice. The times are simulated.
128 devices in a mesh: dp: 16 (over z, y), expert: 8 (over x, core).
Axes of the slice: x: 4, y: 4, z: 4, core: 2. Of those that a mesh axis runs over, the one named last changes fastest.
Arguments:
- tokens: bfloat16 [32768, 768], P(('dp', 'expert')), may hold values from -6 to 6
- w_qkv: bfloat16 [768, 2304], P(('dp', 'expert')), may hold values from -0.21875 to 0.21875
- w_attn_out: bfloat16 [768, 768], P(('dp', 'expert')), may hold values from -1.25 to 1.25
- w_router: bfloat16 [768, 8], P(('dp', 'expert')), may hold values from -0.15625 to 0.15625
- gain_attn: bfloat16 [768], P(('dp', 'expert')), may hold values from 0.5 to 1.5
- gain_moe: bfloat16 [768], P(('dp', 'expert')), may hold values from 0.5 to 1.5
- bias_table: bfloat16 [384], P(('dp', 'expert')), may hold values from -4 to 4
- w_in: bfloat16 [8, 3072, 768], P('expert', 'dp'), may hold values from -0.21875 to 0.21875
- w_out: bfloat16 [8, 3072, 768], P('expert', 'dp'), may hold values from -1.25 to 1.25
- expert_ids: int32 [32768], P(('dp', 'expert')), may hold values from 0 to 7, as said below
- slots: int32 [32768], P(('dp', 'expert')), may hold values from 0 to 16, as said below
- buckets: int32 [128, 128], replicated, may hold values from 0 to 31
- cotangent: float32 [32768, 768], P(('dp', 'expert')), may hold values from -6 to 6
Outputs:
- output: float32 [32768, 768], P(('dp', 'expert'))
- grad_tokens: float32 [32768, 768], P(('dp', 'expert'))
- grad_qkv: float32 [768, 2304], P(('dp', 'expert'))
- grad_attn_out: float32 [768, 768], P(('dp', 'expert'))
- grad_router: float32 [768, 8], P(('dp', 'expert'))
- grad_gain_attn: float32 [768], P(('dp', 'expert'))
- grad_gain_moe: float32 [768], P(('dp', 'expert'))
- grad_bias: float32 [384], P(('dp', 'expert'))
- grad_in: float32 [8, 3072, 768], P('expert', 'dp')
- grad_out: float32 [8, 3072, 768], P('expert', 'dp')
Inputs may be any that keep to these rules, and one draw needn't show every extreme that they name: `expert_ids`: every number names an expert; tokens of one sequence are one block of 128 rows. slots[t] is the number of earlier tokens of t's sequence that name the same expert as t, capped at 16; the value 16 marks a token that its expert drops.
All inputs are finite; a program needn't handle non-finite values.
Results may differ from a plain program's by a relative error of at most 0.029.
Values may be sent and summed in bfloat16 or wider, within the bound.
A program may use at most 192 MiB of HBM per device.

v0:
```python
import jax
import jax.numpy as jnp
from jax import lax
from jax.sharding import PartitionSpec as P

HEAD_DIM = 64
BUCKETS = 32
LEN = 128


NORM_EPS = 1e-06
HIGH_PRECISION = lax.Precision.HIGHEST


def rms_scale(values, gain):
    return values * lax.rsqrt(jnp.mean(values * values, axis=-1, keepdims=True) + NORM_EPS) * gain


def router_gate(router_logits, onehot):
    return jnp.sum(jax.nn.softmax(router_logits, axis=-1) * onehot, axis=-1)


def dispatch_table(route_ids, slot_ids, experts, expert_capacity):
    target = route_ids * expert_capacity + slot_ids
    columns = lax.broadcasted_iota(jnp.int32, (route_ids.shape[0], experts * expert_capacity), 1)
    keep = (target[:, None] == columns) & (slot_ids[:, None] < expert_capacity)
    return keep.astype(jnp.bfloat16)


def expand_bias(bucket_onehot, bias_flat):
    routing_table = bias_flat.astype(jnp.float32).reshape(BUCKETS, -1)
    return jnp.einsum("bij,bh->hij", bucket_onehot, routing_table, precision=HIGH_PRECISION)


def split_heads(query_key_value_rows):
    width = query_key_value_rows.shape[1] // 3
    parts = query_key_value_rows.reshape(
        query_key_value_rows.shape[0], 3, width // HEAD_DIM, HEAD_DIM
    )
    return (parts[:, 0], parts[:, 1], parts[:, 2])


def attention_scores(queries, key_rows, full_bias):
    raw = jnp.einsum("ihc,jhc->hij", queries, key_rows, preferred_element_type=jnp.float32)
    return raw * HEAD_DIM ** (-0.5) + full_bias


def contract_last(left, right):
    return lax.dot_general(
        left, right, (((1,), (1,)), ((), ())), preferred_element_type=jnp.float32
    )


def contract_first(left, right):
    return lax.dot_general(
        left, right, (((0,), (0,)), ((), ())), preferred_element_type=jnp.float32
    )


def local(
    tokens,
    w_qkv,
    w_attn_out,
    w_router,
    gain_attn,
    gain_moe,
    bias_table,
    w_in,
    w_out,
    expert_ids,
    slots,
    buckets,
    cotangent,
):
    experts = lax.axis_size("expert")
    expert_capacity = LEN // experts
    width = tokens.shape[1]
    heads = width // HEAD_DIM
    scale = HEAD_DIM ** (-0.5)
    levels = lax.broadcasted_iota(jnp.int32, (BUCKETS, LEN, LEN), 0)
    bucket_onehot = (levels == buckets[None]).astype(jnp.float32)
    expert_columns = lax.broadcasted_iota(jnp.int32, (LEN, experts), 1)

    def expert_forward(expert_rows):
        piece_in = lax.all_gather(w_in, "dp", axis=1, tiled=True)
        piece_out = lax.all_gather(w_out, "dp", axis=1, tiled=True)
        pre_act = contract_last(expert_rows, piece_in[0])
        hidden_low = jax.nn.gelu(pre_act).astype(jnp.bfloat16)
        return jnp.dot(hidden_low, piece_out[0], preferred_element_type=jnp.float32)

    def expert_backward(expert_rows, rows_grad, sum_in, sum_out):
        acc_in = sum_in
        acc_out = sum_out
        piece_in = lax.all_gather(w_in, "dp", axis=1, tiled=True)
        piece_out = lax.all_gather(w_out, "dp", axis=1, tiled=True)
        pre_act = contract_last(expert_rows, piece_in[0])
        activated, gelu_back = jax.vjp(jax.nn.gelu, pre_act)
        hidden_low = activated.astype(jnp.bfloat16)
        hidden_grad = contract_last(rows_grad, piece_out[0])
        pre_grad = gelu_back(hidden_grad)[0].astype(jnp.bfloat16)
        input_total = jnp.dot(pre_grad, piece_in[0], preferred_element_type=jnp.float32)
        in_piece = contract_first(pre_grad, expert_rows)
        out_piece = contract_first(hidden_low, rows_grad)
        old_in = acc_in
        old_out = acc_out
        acc_in = old_in + in_piece[None]
        acc_out = old_out + out_piece[None]
        return (input_total, acc_in, acc_out)

    def forward_step(carry, blocks):
        x_low, route_ids, slot_ids = blocks
        dense = (
            lax.all_gather(w_qkv, ("dp", "expert"), axis=0, tiled=True),
            lax.all_gather(w_attn_out, ("dp", "expert"), axis=0, tiled=True),
            lax.all_gather(w_router, ("dp", "expert"), axis=0, tiled=True),
            lax.all_gather(gain_attn, ("dp", "expert"), axis=0, tiled=True),
            lax.all_gather(gain_moe, ("dp", "expert"), axis=0, tiled=True),
            lax.all_gather(bias_table, ("dp", "expert"), axis=0, tiled=True),
        )
        wqkv_full, attn_full, router_full, gain_one, gain_two, bias_flat = dense
        full_bias = expand_bias(bucket_onehot, bias_flat)
        x_float = x_low.astype(jnp.float32)
        first_normed = rms_scale(x_float, gain_one.astype(jnp.float32)).astype(jnp.bfloat16)
        query_key_value_rows = jnp.dot(
            first_normed, wqkv_full, preferred_element_type=jnp.float32
        ).astype(jnp.bfloat16)
        queries, key_rows, value_rows = split_heads(query_key_value_rows)
        scores = attention_scores(queries, key_rows, full_bias)
        row_peak = jnp.max(scores, axis=-1, keepdims=True)
        shifted = jnp.exp(scores - row_peak)
        totals = jnp.sum(shifted, axis=-1, keepdims=True)
        attn_low = (shifted / totals).astype(jnp.bfloat16)
        log_norm = row_peak + jnp.log(totals)
        mixed_output = jnp.einsum(
            "hij,jhc->ihc", attn_low, value_rows, preferred_element_type=jnp.float32
        )
        mixed_output = mixed_output.reshape(LEN, width).astype(jnp.bfloat16)
        residual_stream = x_float + jnp.dot(
            mixed_output, attn_full, preferred_element_type=jnp.float32
        )
        second_normed = rms_scale(residual_stream, gain_two.astype(jnp.float32)).astype(
            jnp.bfloat16
        )
        router_logits = jnp.dot(
            second_normed.astype(jnp.float32),
            router_full.astype(jnp.float32),
            precision=HIGH_PRECISION,
        )
        onehot = (route_ids[:, None] == expert_columns).astype(jnp.float32)
        gate = router_gate(router_logits, onehot)
        routing_table = dispatch_table(route_ids, slot_ids, experts, expert_capacity)
        sent_tokens = contract_first(routing_table, second_normed).astype(jnp.bfloat16)
        arrived = lax.all_to_all(
            sent_tokens.reshape(experts, expert_capacity, width),
            "expert",
            split_axis=0,
            concat_axis=0,
            tiled=True,
        )
        arrived = arrived.reshape(experts * expert_capacity, width)
        expert_result = expert_forward(arrived).astype(jnp.bfloat16)
        returned = lax.all_to_all(
            expert_result.reshape(experts, expert_capacity, width),
            "expert",
            split_axis=0,
            concat_axis=0,
            tiled=True,
        )
        combined_output = jnp.dot(
            routing_table,
            returned.reshape(experts * expert_capacity, width),
            preferred_element_type=jnp.float32,
        )
        output = residual_stream + gate[:, None] * combined_output
        return (
            carry,
            (
                output,
                residual_stream,
                log_norm,
                query_key_value_rows,
                mixed_output,
                arrived,
                combined_output,
                gate,
            ),
        )

    def backward_step(grads, blocks):
        (
            x_low,
            route_ids,
            slot_ids,
            cot_rows,
            residual_stream,
            log_norm,
            query_key_value_rows,
            mixed_output,
            arrived,
            combined_output,
            gate,
        ) = blocks
        sum_qkv, sum_attn, sum_router, sum_gain_one, sum_gain_two, sum_bias, sum_in, sum_out = grads
        dense = (
            lax.all_gather(w_qkv, ("dp", "expert"), axis=0, tiled=True),
            lax.all_gather(w_attn_out, ("dp", "expert"), axis=0, tiled=True),
            lax.all_gather(w_router, ("dp", "expert"), axis=0, tiled=True),
            lax.all_gather(gain_attn, ("dp", "expert"), axis=0, tiled=True),
            lax.all_gather(gain_moe, ("dp", "expert"), axis=0, tiled=True),
            lax.all_gather(bias_table, ("dp", "expert"), axis=0, tiled=True),
        )
        wqkv_full, attn_full, router_full, gain_one, gain_two, bias_flat = dense
        full_bias = expand_bias(bucket_onehot, bias_flat)
        routing_table = dispatch_table(route_ids, slot_ids, experts, expert_capacity)
        gate_grad = jnp.sum(cot_rows * combined_output, axis=-1)
        result_grad = (gate[:, None] * cot_rows).astype(jnp.bfloat16)
        sent_grad = contract_first(routing_table, result_grad).astype(jnp.bfloat16)
        arrived_grad = lax.all_to_all(
            sent_grad.reshape(experts, expert_capacity, width),
            "expert",
            split_axis=0,
            concat_axis=0,
            tiled=True,
        )
        arrived_grad = arrived_grad.reshape(experts * expert_capacity, width)
        input_total, sum_in, sum_out = expert_backward(arrived, arrived_grad, sum_in, sum_out)
        back_rows = lax.all_to_all(
            input_total.astype(jnp.bfloat16).reshape(experts, expert_capacity, width),
            "expert",
            split_axis=0,
            concat_axis=0,
            tiled=True,
        )
        from_experts = jnp.dot(
            routing_table,
            back_rows.reshape(experts * expert_capacity, width),
            preferred_element_type=jnp.float32,
        )
        second_normed, norm_two_back = jax.vjp(
            rms_scale, residual_stream, gain_two.astype(jnp.float32)
        )
        normed_float = second_normed.astype(jnp.bfloat16).astype(jnp.float32)
        router_float = router_full.astype(jnp.float32)
        router_logits = jnp.dot(normed_float, router_float, precision=HIGH_PRECISION)
        onehot = (route_ids[:, None] == expert_columns).astype(jnp.float32)

        def gate_of(values):
            return router_gate(values, onehot)

        gate_again, gate_back = jax.vjp(gate_of, router_logits)
        logit_grad = gate_back(gate_grad)[0]
        sum_router = sum_router + jnp.dot(normed_float.T, logit_grad, precision=HIGH_PRECISION)
        normed_grad = jnp.dot(logit_grad, router_float.T, precision=HIGH_PRECISION) + from_experts
        residual_part, gain_two_grad = norm_two_back(normed_grad)
        residual_grad = cot_rows + residual_part
        branch_grad = residual_grad.astype(jnp.bfloat16)
        sum_attn = sum_attn + contract_first(mixed_output, branch_grad)
        mixed_grad = (
            contract_last(branch_grad, attn_full).astype(jnp.bfloat16).reshape(LEN, heads, HEAD_DIM)
        )
        queries, key_rows, value_rows = split_heads(query_key_value_rows)
        scores = attention_scores(queries, key_rows, full_bias)
        attn_float = jnp.exp(scores - log_norm)
        attn_low = attn_float.astype(jnp.bfloat16)
        value_grad = jnp.einsum(
            "hij,ihc->jhc", attn_low, mixed_grad, preferred_element_type=jnp.float32
        )
        prob_grad = jnp.einsum(
            "ihc,jhc->hij", mixed_grad, value_rows, preferred_element_type=jnp.float32
        )
        score_grad = attn_float * (
            prob_grad - jnp.sum(attn_float * prob_grad, axis=-1, keepdims=True)
        )
        sum_bias = sum_bias + jnp.einsum(
            "bij,hij->bh", bucket_onehot, score_grad, precision=HIGH_PRECISION
        )
        score_low = score_grad.astype(jnp.bfloat16)
        query_grad = (
            jnp.einsum("hij,jhc->ihc", score_low, key_rows, preferred_element_type=jnp.float32)
            * scale
        )
        key_grad = (
            jnp.einsum("hij,ihc->jhc", score_low, queries, preferred_element_type=jnp.float32)
            * scale
        )
        qkv_grad = (
            jnp.stack([query_grad, key_grad, value_grad], axis=1)
            .reshape(LEN, 3 * width)
            .astype(jnp.bfloat16)
        )
        x_float = x_low.astype(jnp.float32)
        first_normed, norm_one_back = jax.vjp(rms_scale, x_float, gain_one.astype(jnp.float32))
        sum_qkv = sum_qkv + contract_first(first_normed.astype(jnp.bfloat16), qkv_grad)
        normed_one_grad = contract_last(qkv_grad, wqkv_full)
        input_part, gain_one_grad = norm_one_back(normed_one_grad)
        token_grad = residual_grad + input_part
        updated = (
            sum_qkv,
            sum_attn,
            sum_router,
            sum_gain_one + gain_one_grad,
            sum_gain_two + gain_two_grad,
            sum_bias,
            sum_in,
            sum_out,
        )
        return (updated, token_grad)

    micro_count = tokens.shape[0] // LEN
    token_blocks = tokens.reshape(micro_count, LEN, width)
    route_blocks = expert_ids.reshape(micro_count, LEN)
    slot_blocks = slots.reshape(micro_count, LEN)
    cot_blocks = cotangent.reshape(micro_count, LEN, width)
    unused, stored = lax.scan(
        forward_step, jnp.zeros((), jnp.float32), (token_blocks, route_blocks, slot_blocks)
    )
    (
        outputs,
        residuals,
        log_norms,
        qkv_store,
        mixed_store,
        arrived_store,
        combined_store,
        gate_store,
    ) = stored
    expert_span = w_in.shape[1] * lax.axis_size("dp")
    zero_grads = (
        jnp.zeros((width, 3 * width), jnp.float32),
        jnp.zeros((width, width), jnp.float32),
        jnp.zeros((width, experts), jnp.float32),
        jnp.zeros((width,), jnp.float32),
        jnp.zeros((width,), jnp.float32),
        jnp.zeros((BUCKETS, heads), jnp.float32),
        jnp.zeros((1, expert_span, width), jnp.float32),
        jnp.zeros((1, expert_span, width), jnp.float32),
    )
    final_grads, token_grads = lax.scan(
        backward_step,
        zero_grads,
        (
            token_blocks,
            route_blocks,
            slot_blocks,
            cot_blocks,
            residuals,
            log_norms,
            qkv_store,
            mixed_store,
            arrived_store,
            combined_store,
            gate_store,
        ),
        reverse=True,
    )
    sum_qkv, sum_attn, sum_router, sum_gain_one, sum_gain_two, sum_bias, sum_in, sum_out = (
        final_grads
    )
    grad_in, grad_out = (
        lax.psum_scatter(sum_in.astype(jnp.bfloat16), "dp", scatter_dimension=1, tiled=True).astype(
            jnp.float32
        ),
        lax.psum_scatter(
            sum_out.astype(jnp.bfloat16), "dp", scatter_dimension=1, tiled=True
        ).astype(jnp.float32),
    )
    grad_qkv, grad_attn_out, grad_router, grad_gain_attn, grad_gain_moe, grad_bias = (
        lax.psum_scatter(sum_qkv, ("dp", "expert"), scatter_dimension=0, tiled=True),
        lax.psum_scatter(sum_attn, ("dp", "expert"), scatter_dimension=0, tiled=True),
        lax.psum_scatter(sum_router, ("dp", "expert"), scatter_dimension=0, tiled=True),
        lax.psum_scatter(sum_gain_one, ("dp", "expert"), scatter_dimension=0, tiled=True),
        lax.psum_scatter(sum_gain_two, ("dp", "expert"), scatter_dimension=0, tiled=True),
        lax.psum_scatter(sum_bias.reshape(-1), ("dp", "expert"), scatter_dimension=0, tiled=True),
    )
    output = outputs.reshape(micro_count * LEN, width)
    grad_tokens = token_grads.reshape(micro_count * LEN, width)
    return (
        output,
        grad_tokens,
        grad_qkv,
        grad_attn_out,
        grad_router,
        grad_gain_attn,
        grad_gain_moe,
        grad_bias,
        grad_in,
        grad_out,
    )


def solution(mesh):
    in_specs = (
        P(("dp", "expert"), None),
        P(("dp", "expert"), None),
        P(("dp", "expert"), None),
        P(("dp", "expert"), None),
        P(("dp", "expert")),
        P(("dp", "expert")),
        P(("dp", "expert")),
        P("expert", "dp", None),
        P("expert", "dp", None),
        P(("dp", "expert")),
        P(("dp", "expert")),
        P(),
        P(("dp", "expert"), None),
    )
    out_specs = (
        P(("dp", "expert"), None),
        P(("dp", "expert"), None),
        P(("dp", "expert"), None),
        P(("dp", "expert"), None),
        P(("dp", "expert"), None),
        P(("dp", "expert")),
        P(("dp", "expert")),
        P(("dp", "expert")),
        P("expert", "dp", None),
        P("expert", "dp", None),
    )
    return jax.shard_map(local, mesh=mesh, in_specs=in_specs, out_specs=out_specs, check_vma=False)
```

profile of v0, /device:TPU:1, one launch (start us, length us, event | category | flops | bytes accessed | tf_op | source)
XLA Modules:
  0.0 1842.2 jit_solution(11740135679398198102)
XLA Ops:
  9.0 68.8 %all-reduce.5 = bf16[384]{0:T(512)(128)(2,1)S(1)} all-reduce(bf16[384]{0:T(512)(128)(2,1)S(1)} %dynamic-update-slice.5), channel_id=1, replica_groups=mesh['dp'=16,'expert'=8] {'dp','expert'}, use_global_device_ids=true, to_apply=%add.5 | all-reduce | flops 384 | bytes 1536
  83.3 523.9 %while.58 = (s32[]{:T(128)}, f32[2,128,768]{2,1,0:T(8,128)}, f32[2,128,768]{2,1,0:T(8,128)}, f32[2,12,128,1]{2,1,3,0:T(8,128)}, bf16[2,128,2304]{2,1,0:T(8,128)(...) while((s32[]{:T(128)}, f32[2,128,768]{2,1,0:T(8,128)}, ...), condition=%wide.region_8.9_spmd.clone, body=%wide.region_0.8_spmd.clone.sunk | while | flops 1921820416 | bytes 106024312 | solution.py:314
  87.8 62.9 %all-reduce.25 = (bf16[768]{0:T(1024)(128)(2,1)S(1)}, bf16[768]{0:T(1024)(128)(2,1)S(1)}) all-reduce(bf16[768]{0:T(1024)(128)(2,1)S(1)} %dynamic-update-slice.16, bf16[768]{0:T(1024)(128)(2,1)S(1)} %dynamic-update-slice.17), channel_id=1, replica_groups=mesh['dp'=16,'expert'=8] {'dp','expert'}, use_global_device_ids=true, to_apply=%add | all-reduce | flops 1536 | bytes 6144 | tf_op jit(solution)/shard_map/while
  150.6 33.7 %all-gather.20 = bf16[128,6,8]{2,1,0:T(8,128)(2,1)S(1)} all-gather(bf16[1,6,8]{2,1,0:T(8,128)(2,1)S(1)} %bitcast.453), channel_id=1, replica_groups=mesh['dp'=16,'expert'=8] {'dp','expert'}, dimensions={0}, use_global_device_ids=true | all-gather | bytes 12384 | tf_op jit(solution)/shard_map/while/body/eval_jaxpr/all_gather | solution.py:115
  192.4 23.4 %all-gather.33.cloned.1.call-done = bf16[128,6,2304]{2,1,0:T(8,128)(2,1)} async-done(((bf16[1,6,2304]{2,1,0:T(8,128)(2,1)}), bf16[128,6,2304]{2,1,0:T(8,128)(2,1)}) %all-gather.33.cloned.1.call-update) | async-done | bytes 3538960 | tf_op jit(solution)/shard_map/while/body/eval_jaxpr/all_gather | solution.py:113
  239.5 29.6 %all-gather.37.cloned.1.call-done = bf16[1,3072,768]{2,1,0:T(8,128)(2,1)} async-done(((bf16[1,192,768]{2,1,0:T(8,128)(2,1)}), bf16[1,3072,768]{2,1,0:T(8,128)(2,1)}) %all-gather.37.cloned.1.call-update) | async-done | bytes 4718608 | tf_op jit(solution)/shard_map/while/body/eval_jaxpr/all_gather | solution.py:86
  269.1 55.7 %all-gather.39.cloned.1.call-done = bf16[1,3072,768]{2,1,0:T(8,128)(2,1)} async-done(((bf16[1,192,768]{2,1,0:T(8,128)(2,1)}), bf16[1,3072,768]{2,1,0:T(8,128)(2,1)}) %all-gather.39.cloned.1.call-update) | async-done | bytes 4718608 | tf_op jit(solution)/shard_map/while/body/eval_jaxpr/all_gather | solution.py:85
  349.0 64.6 %all-reduce.25 = (bf16[768]{0:T(1024)(128)(2,1)S(1)}, bf16[768]{0:T(1024)(128)(2,1)S(1)}) all-reduce(bf16[768]{0:T(1024)(128)(2,1)S(1)} %dynamic-update-slice.16, bf16[768]{0:T(1024)(128)(2,1)S(1)} %dynamic-update-slice.17), channel_id=1, replica_groups=mesh['dp'=16,'expert'=8] {'dp','expert'}, use_global_device_ids=true, to_apply=%add | all-reduce | flops 1536 | bytes 6144 | tf_op jit(solution)/shard_map/while
  413.7 34.3 %all-gather.20 = bf16[128,6,8]{2,1,0:T(8,128)(2,1)S(1)} all-gather(bf16[1,6,8]{2,1,0:T(8,128)(2,1)S(1)} %bitcast.453), channel_id=1, replica_groups=mesh['dp'=16,'expert'=8] {'dp','expert'}, dimensions={0}, use_global_device_ids=true | all-gather | bytes 12384 | tf_op jit(solution)/shard_map/while/body/eval_jaxpr/all_gather | solution.py:115
  456.1 22.1 %all-gather.33.cloned.1.call-done = bf16[128,6,2304]{2,1,0:T(8,128)(2,1)} async-done(((bf16[1,6,2304]{2,1,0:T(8,128)(2,1)}), bf16[128,6,2304]{2,1,0:T(8,128)(2,1)}) %all-gather.33.cloned.1.call-update) | async-done | bytes 3538960 | tf_op jit(solution)/shard_map/while/body/eval_jaxpr/all_gather | solution.py:113
  501.9 29.6 %all-gather.37.cloned.1.call-done = bf16[1,3072,768]{2,1,0:T(8,128)(2,1)} async-done(((bf16[1,192,768]{2,1,0:T(8,128)(2,1)}), bf16[1,3072,768]{2,1,0:T(8,128)(2,1)}) %all-gather.37.cloned.1.call-update) | async-done | bytes 4718608 | tf_op jit(solution)/shard_map/while/body/eval_jaxpr/all_gather | solution.py:86
  531.5 55.9 %all-gather.39.cloned.1.call-done = bf16[1,3072,768]{2,1,0:T(8,128)(2,1)} async-done(((bf16[1,192,768]{2,1,0:T(8,128)(2,1)}), bf16[1,3072,768]{2,1,0:T(8,128)(2,1)}) %all-gather.39.cloned.1.call-update) | async-done | bytes 4718608 | tf_op jit(solution)/shard_map/while/body/eval_jaxpr/all_gather | solution.py:85
  608.2 578.0 %while.59 = (s32[]{:T(128)}, f32[768,2304]{1,0:T(8,128)}, f32[768,768]{1,0:T(8,128)}, f32[768,8]{0,1:T(8,128)}, f32[768]{0:T(1024)}, /*index=5*/f32[768]{0:T(102...) while((s32[]{:T(128)}, f32[768,2304]{1,0:T(8,128)}, ...), condition=%wide.region_21.22_spmd.clone, body=%wide.region_9.21_spmd.clone.sunk | while | flops 4611185664 | bytes 251209872 | solution.py:338
  622.1 65.0 %all-reduce.26 = (bf16[768]{0:T(1024)(128)(2,1)S(1)}, bf16[384]{0:T(512)(128)(2,1)S(1)}, bf16[768]{0:T(1024)(128)(2,1)S(1)}) all-reduce(bf16[768]{0:T(1024)(128)(2,1)S(1)} %dynamic-update-slice.18, bf16[384]{0:T(512)(128)(2,1)S(1)} %dynamic-update-slice.19, ...), channel_id=1, replica_groups=mesh['dp'=16,'expert'=8] {'dp','expert'}, use_global_device_ids=true, to_apply=%add.4 | all-reduce | flops 1920 | bytes 7680 | tf_op jit(solution)/shard_map/while
  687.0 33.9 %all-gather.22 = bf16[128,6,8]{2,1,0:T(8,128)(2,1)S(1)} all-gather(bf16[1,6,8]{2,1,0:T(8,128)(2,1)S(1)} %bitcast.454), channel_id=1, replica_groups=mesh['dp'=16,'expert'=8] {'dp','expert'}, dimensions={0}, use_global_device_ids=true | all-gather | bytes 12384 | tf_op jit(solution)/shard_map/while/body/eval_jaxpr/all_gather | solution.py:207
  748.9 46.7 %all-gather.43.cloned.1.call-done = bf16[1,3072,768]{2,1,0:T(8,128)(2,1)} async-done(((bf16[1,192,768]{2,1,0:T(8,128)(2,1)}), bf16[1,3072,768]{2,1,0:T(8,128)(2,1)}) %all-gather.43.cloned.1.call-update) | async-done | bytes 4718608 | tf_op jit(solution)/shard_map/while/body/eval_jaxpr/all_gather | solution.py:94
  799.7 51.6 %all-gather.45.cloned.1.call-done = bf16[1,3072,768]{2,1,0:T(8,128)(2,1)} async-done(((bf16[1,192,768]{2,1,0:T(8,128)(2,1)}), bf16[1,3072,768]{2,1,0:T(8,128)(2,1)}) %all-gather.45.cloned.1.call-update) | async-done | bytes 4718608 | tf_op jit(solution)/shard_map/while/body/eval_jaxpr/all_gather | solution.py:95
  905.7 65.2 %all-reduce.26 = (bf16[768]{0:T(1024)(128)(2,1)S(1)}, bf16[384]{0:T(512)(128)(2,1)S(1)}, bf16[768]{0:T(1024)(128)(2,1)S(1)}) all-reduce(bf16[768]{0:T(1024)(128)(2,1)S(1)} %dynamic-update-slice.18, bf16[384]{0:T(512)(128)(2,1)S(1)} %dynamic-update-slice.19, ...), channel_id=1, replica_groups=mesh['dp'=16,'expert'=8] {'dp','expert'}, use_global_device_ids=true, to_apply=%add.4 | all-reduce | flops 1920 | bytes 7680 | tf_op jit(solution)/shard_map/while
  970.9 33.7 %all-gather.22 = bf16[128,6,8]{2,1,0:T(8,128)(2,1)S(1)} all-gather(bf16[1,6,8]{2,1,0:T(8,128)(2,1)S(1)} %bitcast.454), channel_id=1, replica_groups=mesh['dp'=16,'expert'=8] {'dp','expert'}, dimensions={0}, use_global_device_ids=true | all-gather | bytes 12384 | tf_op jit(solution)/shard_map/while/body/eval_jaxpr/all_gather | solution.py:207
  1033.6 46.5 %all-gather.43.cloned.1.call-done = bf16[1,3072,768]{2,1,0:T(8,128)(2,1)} async-done(((bf16[1,192,768]{2,1,0:T(8,128)(2,1)}), bf16[1,3072,768]{2,1,0:T(8,128)(2,1)}) %all-gather.43.cloned.1.call-update) | async-done | bytes 4718608 | tf_op jit(solution)/shard_map/while/body/eval_jaxpr/all_gather | solution.py:94
  1084.3 51.6 %all-gather.45.cloned.1.call-done = bf16[1,3072,768]{2,1,0:T(8,128)(2,1)} async-done(((bf16[1,192,768]{2,1,0:T(8,128)(2,1)}), bf16[1,3072,768]{2,1,0:T(8,128)(2,1)}) %all-gather.45.cloned.1.call-update) | async-done | bytes 4718608 | tf_op jit(solution)/shard_map/while/body/eval_jaxpr/all_gather | solution.py:95
  1200.7 360.0 %fusion.166 = (f32[8,2304]{1,0:T(8,128)S(1)}, f32[8,768]{1,0:T(8,128)S(1)}) fusion(f32[768,2304]{1,0:T(8,128)} %get-tuple-element.877, f32[768,768]{1,0:T(8,128)S(1)} %copy-done.5), kind=kCustom, calls=%all-reduce-scatter.2 | all-reduce-scatter fusion | flops 3145729 | bytes 9535488
  1703.1 66.5 %all-reduce.21 = (f32[768,8]{1,0:T(8,128)S(1)}, f32[768]{0:T(1024)S(1)}, f32[768]{0:T(1024)S(1)}, f32[384]{0:T(512)S(1)}) all-reduce(f32[768,8]{1,0:T(8,128)S(1)} %copy.73, f32[768]{0:T(1024)S(1)} %copy-done.41, f32[768]{0:T(1024)S(1)} %copy-done.44, f32[384]{0:T(512)S(1)} %reshape.365), channel_id=4, replica_groups=mesh['dp'=16,'expert'=8] {'dp','expert'}, use_global_device_ids=true, to_apply=%region_24.25.clone | all-reduce | flops 8064 | bytes 64512
  1810.3 20.3 %concatenate = f32[262,2304]{1,0:T(8,128)S(1)} concatenate(f32[6,2304]{1,0:T(8,128)S(1)} %collective-permute-done.31, f32[8,2304]{1,0:T(8,128)S(1)} %collective-permute-done.30, f32[8,2304]{1,0:T(8,128)S(1)} %collective-permute-done.29, f32[8,2304]{1,0:T(8,128)S(1)} %collective-permute-done.28, f32[8,2304]{1,0:T(8,128)S(1)} %collective-permute-done.27, ...), dimensions={0} | concatenate | bytes 4829184
  (680 shorter events, 501.5 us)
Async XLA Ops:
  83.3 105.9 %all-gather.35.cloned.1.call-start = ((), (), s32[]{:S(2)}) async-start(), calls=%async_computation.9 | async-start | bytes 1585152 | tf_op jit(solution)/shard_map/while/body/eval_jaxpr/all_gather | solution.py:114
  84.0 131.7 %all-gather.33.cloned.1.call-start = ((), (), s32[]{:S(2)}) async-start(), calls=%async_computation.8 | async-start | bytes 4755456 | tf_op jit(solution)/shard_map/while/body/eval_jaxpr/all_gather | solution.py:113
  84.8 184.3 %all-gather.37.cloned.1.call-start = ((), (), s32[]{:S(2)}) async-start(), calls=%async_computation.10 | async-start | bytes 5013504 | tf_op jit(solution)/shard_map/while/body/eval_jaxpr/all_gather | solution.py:86
  85.5 239.3 %all-gather.39.cloned.1.call-start = ((), (), s32[]{:S(2)}) async-start(), calls=%async_computation.11 | async-start | bytes 5013504 | tf_op jit(solution)/shard_map/while/body/eval_jaxpr/all_gather | solution.py:85
  344.7 108.2 %all-gather.35.cloned.1.call-start = ((), (), s32[]{:S(2)}) async-start(), calls=%async_computation.9 | async-start | bytes 1585152 | tf_op jit(solution)/shard_map/while/body/eval_jaxpr/all_gather | solution.py:114
  345.2 133.0 %all-gather.33.cloned.1.call-start = ((), (), s32[]{:S(2)}) async-start(), calls=%async_computation.8 | async-start | bytes 4755456 | tf_op jit(solution)/shard_map/while/body/eval_jaxpr/all_gather | solution.py:113
  345.8 185.7 %all-gather.37.cloned.1.call-start = ((), (), s32[]{:S(2)}) async-start(), calls=%async_computation.10 | async-start | bytes 5013504 | tf_op jit(solution)/shard_map/while/body/eval_jaxpr/all_gather | solution.py:86
  346.6 240.8 %all-gather.39.cloned.1.call-start = ((), (), s32[]{:S(2)}) async-start(), calls=%async_computation.11 | async-start | bytes 5013504 | tf_op jit(solution)/shard_map/while/body/eval_jaxpr/all_gather | solution.py:85
  608.5 123.4 %all-gather.41.cloned.1.call-start = ((), (), s32[]{:S(2)}) async-start(), calls=%async_computation.12 | async-start | bytes 1585152 | tf_op jit(solution)/shard_map/while/body/eval_jaxpr/all_gather | solution.py:206
  609.3 133.0 %all-gather.47.cloned.1.call-start = ((), (), s32[]{:S(2)}) async-start(), calls=%async_computation.15 | async-start | bytes 4755456 | tf_op jit(solution)/shard_map/while/body/eval_jaxpr/all_gather | solution.py:205
  609.9 185.7 %all-gather.43.cloned.1.call-start = ((), (), s32[]{:S(2)}) async-start(), calls=%async_computation.13 | async-start | bytes 5013504 | tf_op jit(solution)/shard_map/while/body/eval_jaxpr/all_gather | solution.py:94
  610.6 240.7 %all-gather.45.cloned.1.call-start = ((), (), s32[]{:S(2)}) async-start(), calls=%async_computation.14 | async-start | bytes 5013504 | tf_op jit(solution)/shard_map/while/body/eval_jaxpr/all_gather | solution.py:95
  615.3 184.5 %all-to-all-start.2 = ((bf16[8,16,768]{2,1,0:T(8,128)(2,1)}), bf16[8,16,768]{2,1,0:T(8,128)(2,1)S(1)}, u32[]{:S(2)}, u32[]{:S(2)}) async-start(bf16[8,16,768]{2,1,0:T(8,128)(2,1)} %bitcast.422), calls=%async_computation.2 | async-start | bytes 393216 | tf_op jit(solution)/shard_map/while/body/eval_jaxpr/all_to_all | solution.py:218
  891.8 123.9 %all-gather.41.cloned.1.call-start = ((), (), s32[]{:S(2)}) async-start(), calls=%async_computation.12 | async-start | bytes 1585152 | tf_op jit(solution)/shard_map/while/body/eval_jaxpr/all_gather | solution.py:206
  892.5 134.5 %all-gather.47.cloned.1.call-start = ((), (), s32[]{:S(2)}) async-start(), calls=%async_computation.15 | async-start | bytes 4755456 | tf_op jit(solution)/shard_map/while/body/eval_jaxpr/all_gather | solution.py:205
  893.1 187.0 %all-gather.43.cloned.1.call-start = ((), (), s32[]{:S(2)}) async-start(), calls=%async_computation.13 | async-start | bytes 5013504 | tf_op jit(solution)/shard_map/while/body/eval_jaxpr/all_gather | solution.py:94
  893.7 242.1 %all-gather.45.cloned.1.call-start = ((), (), s32[]{:S(2)}) async-start(), calls=%async_computation.14 | async-start | bytes 5013504 | tf_op jit(solution)/shard_map/while/body/eval_jaxpr/all_gather | solution.py:95
  898.4 185.9 %all-to-all-start.2 = ((bf16[8,16,768]{2,1,0:T(8,128)(2,1)}), bf16[8,16,768]{2,1,0:T(8,128)(2,1)S(1)}, u32[]{:S(2)}, u32[]{:S(2)}) async-start(bf16[8,16,768]{2,1,0:T(8,128)(2,1)} %bitcast.422), calls=%async_computation.2 | async-start | bytes 393216 | tf_op jit(solution)/shard_map/while/body/eval_jaxpr/all_to_all | solution.py:218
  1186.1 645.1 %reduce-scatter.7.cloned.1.call-start = ((), (), s32[]{:S(2)}) async-start(), calls=%async_computation.6 | async-start | bytes 5013504 | tf_op jit(solution)/shard_map/reduce_scatter | solution.py:360
  1192.6 640.4 %reduce-scatter.9.cloned.1.call-start = ((), (), s32[]{:S(2)}) async-start(), calls=%async_computation.7 | async-start | bytes 5013504 | tf_op jit(solution)/shard_map/reduce_scatter | solution.py:363
  1686.9 84.4 %collective-permute-start.14 = (f32[8,2304]{1,0:T(8,128)S(1)}, f32[8,2304]{1,0:T(8,128)S(1)}, u32[]{:S(2)}, u32[]{:S(2)}) collective-permute-start(f32[8,2304]{1,0:T(8,128)S(1)} %get-tuple-element.1290), channel_id=1, source_target_pairs={{0,15},{1,16},{2,17},{3,18},{4,19},{5,20},{6,21},{7,22},{8,23},{9,... | collective-permute-start | bytes 221192
  1691.8 83.7 %collective-permute-start.12 = (f32[8,2304]{1,0:T(8,128)S(1)}, f32[8,2304]{1,0:T(8,128)S(1)}, u32[]{:S(2)}, u32[]{:S(2)}) collective-permute-start(f32[8,2304]{1,0:T(8,128)S(1)} %get-tuple-element.1290), channel_id=1, source_target_pairs={{0,13},{1,14},{2,15},{3,16},{4,17},{5,18},{6,19},{7,20},{8,21},{9,... | collective-permute-start | bytes 221192
  1695.0 84.4 %collective-permute-start.11 = (f32[8,2304]{1,0:T(8,128)S(1)}, f32[8,2304]{1,0:T(8,128)S(1)}, u32[]{:S(2)}, u32[]{:S(2)}) collective-permute-start(f32[8,2304]{1,0:T(8,128)S(1)} %get-tuple-element.1290), channel_id=1, source_target_pairs={{0,12},{1,13},{2,14},{3,15},{4,16},{5,17},{6,18},{7,19},{8,20},{9,... | collective-permute-start | bytes 221192
  1697.6 85.8 %collective-permute-start.10 = (f32[8,2304]{1,0:T(8,128)S(1)}, f32[8,2304]{1,0:T(8,128)S(1)}, u32[]{:S(2)}, u32[]{:S(2)}) collective-permute-start(f32[8,2304]{1,0:T(8,128)S(1)} %get-tuple-element.1290), channel_id=1, source_target_pairs={{0,11},{1,12},{2,13},{3,14},{4,15},{5,16},{6,17},{7,18},{8,19},{9,... | collective-permute-start | bytes 221192
  (203 other events, 5045.0 us)
Sparse Core Ops, SparseCore 0:
  86.9 61.0 all-gather.34
  151.0 64.7 all-gather.32
  217.9 51.1 all-gather.36
  271.1 53.6 all-gather.38
  348.0 62.7 all-gather.34
  413.6 64.5 all-gather.32
  480.3 51.1 all-gather.36
  533.7 53.6 all-gather.38
  612.2 62.6 all-gather.40
  677.7 64.4 all-gather.46
  744.4 51.1 all-gather.42
  797.6 53.6 all-gather.44
  895.4 64.1 all-gather.40
  962.5 64.4 all-gather.46
  1029.0 51.0 all-gather.42
  1082.1 53.6 all-gather.44
Sparse Core Ops, SparseCore 1:
  1192.7 81.6 reduce-scatter.6
  1277.6 82.7 reduce-scatter.8
where the time goes:
time: 1860 us; the launch traced here: 1840 us
  blocking collectives  888 us (48%)
  waiting for transfers between devices  462 us (25%)
  starting transfers between devices  210 us (11%)
  matrix products  124 us (7%)
  local copies, waits for them, and re-layouts  99.3 us (5%)
  other arithmetic  38.7 us (2%)
    unnamed x3, blocking collectives  495 us
    while x4, blocking collectives  258 us
    unnamed x64, starting transfers between devices  174 us
    all_gather x2, waiting for transfers between devices, expert_forward(): piece_in = lax.all_gather(w_in, 'dp', axis=1, tiled=True)  112 us
    all_gather x2, waiting for transfers between devices, expert_backward(): piece_out = lax.all_gather(w_out, 'dp', axis=1, tiled=True)  103 us
    all_gather x2, waiting for transfers between devices, expert_backward(): piece_in = lax.all_gather(w_in, 'dp', axis=1, tiled=True)  93.3 us
    all_gather x2, blocking collectives, forward_step(): lax.all_gather(w_router, ('dp', 'expert'), axis=0, tiled=True)  68 us
    all_gather x2, blocking collectives, backward_step(): lax.all_gather(w_router, ('dp', 'expert'), axis=0, tiled=True)  67.6 us
  transfers between devices with their start and end apart: 90, of which 16 were waited for; matrix products, arithmetic and copies ran while one was open for 29% of the time, Pallas kernels for 0%

commit v1 on v0

v1 whole, which is shorter than its diff:
```python
import functools

import jax
import jax.numpy as jnp
import numpy as np
from jax import lax
from jax.experimental import pallas as pl
from jax.experimental.pallas import tpu as pltpu
from jax.sharding import PartitionSpec as P

MESH = pl.DeviceIdType.MESH
HEADS = 12
HEAD_DIM = 64
BUCKETS = 32
LEN = 128
WIDTH = 768
FF = 3072
EXPERTS = 8
DP = 16
CAP = 16
SHARD = FF // DP
COLS = 384
ROWS = 48
NORM_EPS = 1e-06
HIGH = lax.Precision.HIGHEST
F32 = jnp.float32
BF16 = jnp.bfloat16
MIB = 1 << 20


def place_matrix():
    m = np.zeros((160, 384), np.float32)
    for c in range(3):
        for e in range(8):
            for r in range(6):
                m[c * 48 + e * 6 + r, e * 48 + c * 6 + r] = 1
    for e in range(8):
        m[144 + e, e * 48 + 32] = 1
    return m


def spread_matrix():
    m = np.zeros((256, 144), np.float32)
    for c in range(3):
        for e in range(8):
            for r in range(6):
                m[e * 32 + c * 6 + r, c * 48 + e * 6 + r] = 1
    return m


class Where:
    def __init__(self):
        self.dp = lax.axis_index("dp")
        self.e = lax.axis_index("expert")
        self.z, self.y = lax.div(self.dp, 4), lax.rem(self.dp, 4)
        self.x, self.c = lax.div(self.e, 2), lax.rem(self.e, 2)
        self.partner_e = self.x * 2 + (1 - self.c)
        self.partner = {"expert": self.partner_e}

    def at(self, axis, step):
        if axis == "y":
            return self.z * 4 + lax.rem(self.y + step + 4, 4)
        if axis == "z":
            return lax.rem(self.z + step + 4, 4) * 4 + self.y
        return lax.rem(self.x + step + 4, 4) * 2 + self.c

    def dev(self, axis, step):
        return {"expert" if axis == "x" else "dp": self.at(axis, step)}

    def at2(self, axis1, step1, step2):
        dy, dz = (step1, step2) if axis1 == "y" else (step2, step1)
        return lax.rem(self.z + dz + 4, 4) * 4 + lax.rem(self.y + dy + 4, 4)


def greet(w, dp_too):
    barrier = pltpu.get_barrier_semaphore()

    def hello_e(k, n):
        pl.semaphore_signal(
            barrier, inc=1, device_id={"expert": lax.rem(w.e + k, EXPERTS)}, device_id_type=MESH
        )
        return n

    def hello_dp(k, n):
        pl.semaphore_signal(
            barrier, inc=1, device_id={"dp": lax.rem(w.dp + k, DP)}, device_id_type=MESH
        )
        return n

    lax.fori_loop(1, EXPERTS, hello_e, 0)
    if dp_too:
        lax.fori_loop(1, DP, hello_dp, 0)
    pl.semaphore_wait(barrier, EXPERTS - 1 + (DP - 1 if dp_too else 0))


def remote(src, dst, send, recv, dev):
    return pltpu.make_async_remote_copy(
        src_ref=src, dst_ref=dst, send_sem=send, recv_sem=recv, device_id=dev, device_id_type=MESH
    )


class RingGather:
    def __init__(self, w, axis, place, rows, send, recv, base, own=None):
        self.w, self.axis, self.place, self.half = w, axis, place, rows // 2
        self.send, self.recv, self.base = send, recv, base
        self.own = place(0) if own is None else own
        self.copies = []

    def _go(self, k, src, dst, step):
        copy = remote(
            src,
            dst,
            self.send.at[self.base + k],
            self.recv.at[self.base + k],
            self.w.dev(self.axis, step),
        )
        copy.start()
        self.copies.append(copy)

    def start(self):
        self._go(0, self.own, self.place(0), 1)
        self._go(1, self.own, self.place(0), -1)

    def relay(self):
        h = self.half
        self.copies[0].wait_recv()
        low = self.place(-1).at[pl.ds(0, h)]
        self._go(2, low, low, 1)
        self.copies[1].wait_recv()
        high = self.place(1).at[pl.ds(h, h)]
        self._go(3, high, high, -1)

    def finish(self):
        self.copies[2].wait_recv()
        self.copies[3].wait_recv()

    def drain(self):
        for copy in self.copies:
            copy.wait_send()


def gather_kernel(
    win_ref,
    wout_ref,
    first_ref,
    place_ref,
    in_ref,
    out_ref,
    dense_ref,
    extra_ref,
    got,
    piece,
    extra_piece,
    own_sem,
    a2a_send,
    a2a_recv,
    dp_send,
    dp_recv,
    ring_send,
    ring_recv,
    x_send,
    x_recv,
):
    w = Where()
    greet(w, True)

    def to_expert(k):
        peer = lax.rem(w.e + k, EXPERTS)
        return remote(
            first_ref.at[peer], got.at[w.e], a2a_send.at[k], a2a_recv.at[k], {"expert": peer}
        )

    def start_a2a(k, n):
        to_expert(k).start()
        return n

    lax.fori_loop(1, EXPERTS, start_a2a, 0)
    got[w.e] = first_ref[w.e]

    keep_in = pltpu.make_async_copy(win_ref, in_ref.at[w.dp], own_sem.at[0])
    keep_out = pltpu.make_async_copy(wout_ref, out_ref.at[w.dp], own_sem.at[1])
    keep_in.start()
    keep_out.start()
    one, two = {}, {}
    for n, (ref, own, axis1, axis2) in enumerate(
        ((in_ref, win_ref, "y", "z"), (out_ref, wout_ref, "z", "y"))
    ):
        one[n] = RingGather(
            w,
            axis1,
            lambda s, ref=ref, a=axis1: ref.at[w.at2(a, s, 0)],
            SHARD,
            ring_send,
            ring_recv,
            n * 20,
            own=own,
        )
        for k, o in enumerate((0, -1, 1, 2)):
            two[n, o] = RingGather(
                w,
                axis2,
                lambda s, ref=ref, a=axis1, o=o: ref.at[w.at2(a, o, s)],
                SHARD,
                ring_send,
                ring_recv,
                n * 20 + 4 + 4 * k,
                own=own if o == 0 else None,
            )
    for n in range(2):
        one[n].start()
    for n in range(2):
        two[n, 0].start()

    def end_a2a(k, n):
        copy = to_expert(k)
        copy.wait_recv()
        copy.wait_send()
        return n

    lax.fori_loop(1, EXPERTS, end_a2a, 0)
    placed = jnp.dot(place_ref[...], got[...].reshape(384, 128), preferred_element_type=F32).astype(
        BF16
    )
    for c in range(3):
        piece[:, c * 128 : (c + 1) * 128] = placed[c * 48 : (c + 1) * 48]
    extra_piece[...] = placed[144:160]
    mine = pl.ds(pl.multiple_of(w.dp * ROWS, 16), ROWS)
    keep_piece = pltpu.make_async_copy(piece, dense_ref.at[w.e, mine], own_sem.at[2])
    keep_extra = pltpu.make_async_copy(extra_piece, extra_ref.at[w.dp], own_sem.at[3])
    keep_piece.start()
    keep_extra.start()

    def to_dp(k):
        dev = {"dp": lax.rem(w.dp + k, DP)}
        return (
            remote(piece, dense_ref.at[w.e, mine], dp_send.at[0, k], dp_recv.at[0, k], dev),
            remote(extra_piece, extra_ref.at[w.dp], dp_send.at[1, k], dp_recv.at[1, k], dev),
        )

    def start_dp(k, n):
        for copy in to_dp(k):
            copy.start()
        return n

    def end_dp(k, n):
        for copy in to_dp(k):
            copy.wait_recv()
            copy.wait_send()
        return n

    lax.fori_loop(1, DP, start_dp, 0)
    for n in range(2):
        one[n].relay()
        two[n, -1].start()
        two[n, 1].start()
    lax.fori_loop(1, DP, end_dp, 0)
    keep_piece.wait()
    ring = RingGather(w, "x", lambda s: dense_ref.at[w.at("x", s)], WIDTH, x_send, x_recv, 0)
    ring.start()

    def across(k, ref):
        copy = remote(ref, ref, x_send.at[4 + k], x_recv.at[4 + k], w.partner)
        copy.start()
        return copy

    pair = [across(0, dense_ref.at[w.e])]
    for n in range(2):
        two[n, 0].relay()
    for n in range(2):
        one[n].finish()
        two[n, 2].start()
    ring.relay()
    pair.append(across(1, dense_ref.at[w.at("x", -1)]))
    pair.append(across(2, dense_ref.at[w.at("x", 1)]))
    for n in range(2):
        two[n, -1].relay()
        two[n, 1].relay()
    ring.finish()
    pair.append(across(3, dense_ref.at[w.at("x", 2)]))
    for n in range(2):
        two[n, 2].relay()
    for n in range(2):
        for o in (0, -1, 1, 2):
            two[n, o].finish()
    for copy in pair:
        copy.wait_recv()
        copy.wait_send()
    ring.drain()
    for n in range(2):
        one[n].drain()
        for o in (0, -1, 1, 2):
            two[n, o].drain()
    keep_in.wait()
    keep_out.wait()
    keep_extra.wait()


def gather(win, wout, first):
    hbm = pl.BlockSpec(memory_space=pl.ANY)
    vmem = pl.BlockSpec(memory_space=pltpu.VMEM)
    return pl.pallas_call(
        gather_kernel,
        out_shape=(
            jax.ShapeDtypeStruct((DP, SHARD, WIDTH), BF16),
            jax.ShapeDtypeStruct((DP, SHARD, WIDTH), BF16),
            jax.ShapeDtypeStruct((EXPERTS, WIDTH, COLS), BF16),
            jax.ShapeDtypeStruct((DP, 16, 128), BF16),
        ),
        in_specs=[hbm, hbm, vmem, vmem],
        out_specs=(hbm, hbm, hbm, hbm),
        scratch_shapes=[
            pltpu.VMEM((EXPERTS, 48, 128), BF16),
            pltpu.VMEM((ROWS, COLS), BF16),
            pltpu.VMEM((16, 128), BF16),
            pltpu.SemaphoreType.DMA((4,)),
            pltpu.SemaphoreType.DMA((EXPERTS,)),
            pltpu.SemaphoreType.DMA((EXPERTS,)),
            pltpu.SemaphoreType.DMA((2, DP)),
            pltpu.SemaphoreType.DMA((2, DP)),
            pltpu.SemaphoreType.DMA((40,)),
            pltpu.SemaphoreType.DMA((40,)),
            pltpu.SemaphoreType.DMA((8,)),
            pltpu.SemaphoreType.DMA((8,)),
        ],
        compiler_params=pltpu.CompilerParams(
            collective_id=0, has_side_effects=True, vmem_limit_bytes=32 * MIB
        ),
        name="gather_weights",
    )(win, wout, first, jnp.asarray(place_matrix(), BF16))


def exchange_kernel(src_ref, dst_ref, own_sem, send, recv):
    w = Where()
    greet(w, False)

    def to(k):
        peer = lax.rem(w.e + k, EXPERTS)
        return remote(src_ref.at[peer], dst_ref.at[w.e], send.at[k], recv.at[k], {"expert": peer})

    def begin(k, n):
        to(k).start()
        return n

    def end(k, n):
        copy = to(k)
        copy.wait_recv()
        copy.wait_send()
        return n

    lax.fori_loop(1, EXPERTS, begin, 0)
    keep = pltpu.make_async_copy(src_ref.at[w.e], dst_ref.at[w.e], own_sem)
    keep.start()
    lax.fori_loop(1, EXPERTS, end, 0)
    keep.wait()


def exchange(blocks, number, name):
    hbm = pl.BlockSpec(memory_space=pl.ANY)
    return pl.pallas_call(
        exchange_kernel,
        out_shape=jax.ShapeDtypeStruct(blocks.shape, blocks.dtype),
        in_specs=[hbm],
        out_specs=hbm,
        scratch_shapes=[
            pltpu.SemaphoreType.DMA,
            pltpu.SemaphoreType.DMA((EXPERTS,)),
            pltpu.SemaphoreType.DMA((EXPERTS,)),
        ],
        compiler_params=pltpu.CompilerParams(collective_id=number, has_side_effects=True),
        name=name,
    )(blocks)


def add_rows(rows, step, dst, *srcs):
    def body(i, n):
        part = pl.ds(pl.multiple_of(i * step, step), step)
        total = srcs[0][part].astype(F32)
        for src in srcs[1:]:
            total = total + src[part].astype(F32)
        dst[part] = total.astype(dst.dtype)
        return n

    lax.fori_loop(0, rows // step, body, 0)


class RingSum:
    def __init__(self, w, axis, place, rows, relayed, landed, send, recv, base):
        self.w, self.axis, self.place, self.rows, self.half = w, axis, place, rows, rows // 2
        self.relayed, self.landed = relayed, landed
        self.send, self.recv, self.base = send, recv, base
        self.copies = {}

    def _go(self, k, src, dst, step):
        copy = remote(
            src,
            dst,
            self.send.at[self.base + k],
            self.recv.at[self.base + k],
            self.w.dev(self.axis, step),
        )
        copy.start()
        self.copies[k] = copy

    def _part(self, ref, k):
        return ref.at[pl.ds(k * self.half, self.half)]

    def far(self):
        self._go(0, self._part(self.place(2), 0), self.relayed.at[0], 1)
        self._go(1, self._part(self.place(2), 1), self.relayed.at[1], -1)

    def near(self):
        self._go(2, self._part(self.place(1), 1), self._part(self.landed.at[0], 1), 1)
        self._go(3, self._part(self.place(-1), 0), self._part(self.landed.at[1], 0), -1)

    def relay(self):
        self.copies[0].wait_recv()
        low = self._part(self.place(1), 0)
        add_rows(self.half, 32, low, low, self.relayed.at[0])
        self._go(4, low, self._part(self.landed.at[0], 0), 1)
        self.copies[1].wait_recv()
        high = self._part(self.place(-1), 1)
        add_rows(self.half, 32, high, high, self.relayed.at[1])
        self._go(5, high, self._part(self.landed.at[1], 1), -1)

    def finish(self, dst):
        for k in (2, 3, 4, 5):
            self.copies[k].wait_recv()
        add_rows(self.rows, 32, dst, self.place(0), self.landed.at[0], self.landed.at[1])

    def drain(self):
        for k in range(6):
            self.copies[k].wait_send()


def reduce_kernel(
    gin_ref,
    gout_ref,
    dense_ref,
    extra_ref,
    spread_ref,
    in_ref,
    out_ref,
    dense_out_ref,
    extra_out_ref,
    grads,
    relayed,
    landed,
    dense,
    crossed,
    x_relayed,
    x_landed,
    dp_got,
    dp_extra,
    extra_sum,
    last,
    last_got,
    extra_got,
    own_sem,
    ring_send,
    ring_recv,
    x_send,
    x_recv,
    dp_send,
    dp_recv,
    a2a_send,
    a2a_recv,
):
    w = Where()
    load_in = pltpu.make_async_copy(gin_ref, grads.at[0], own_sem.at[0])
    load_out = pltpu.make_async_copy(gout_ref, grads.at[1], own_sem.at[1])
    load_dense = pltpu.make_async_copy(dense_ref, dense, own_sem.at[2])
    load_in.start()
    load_out.start()
    load_dense.start()
    greet(w, True)
    axes = (("y", "z"), ("z", "y"))
    order = (2, 1, -1, 0)
    one, two = {}, {}
    for n, (axis1, axis2) in enumerate(axes):
        for k, o in enumerate(order):
            two[n, o] = RingSum(
                w,
                axis2,
                lambda s, n=n, a=axis1, o=o: grads.at[n, w.at2(a, o, s)],
                SHARD,
                relayed.at[n * 5 + k],
                landed.at[n * 5 + k],
                ring_send,
                ring_recv,
                (n * 5 + k) * 6,
            )
        one[n] = RingSum(
            w,
            axis1,
            lambda s, n=n, a=axis1: grads.at[n, w.at2(a, s, 0)],
            SHARD,
            relayed.at[n * 5 + 4],
            landed.at[n * 5 + 4],
            ring_send,
            ring_recv,
            (n * 5 + 4) * 6,
        )
    load_in.wait()
    load_out.wait()
    for n in range(2):
        two[n, 2].far()
    for n in range(2):
        for o in (1, -1, 0):
            two[n, o].far()
    for n in range(2):
        two[n, 2].near()
    for n in range(2):
        for o in (1, -1, 0):
            two[n, o].near()
    load_dense.wait()
    pair = []
    for k in range(4):
        copy = remote(
            dense.at[2 * k + 1 - w.c],
            crossed.at[k],
            x_send.at[6 + k],
            x_recv.at[6 + k],
            w.partner,
        )
        copy.start()
        pair.append(copy)

    def extra_dp(k):
        peer = lax.rem(w.dp + k, DP)
        return remote(
            extra_ref.at[peer], dp_extra.at[w.dp], dp_send.at[1, k], dp_recv.at[1, k], {"dp": peer}
        )

    def start_extra(k, n):
        extra_dp(k).start()
        return n

    lax.fori_loop(1, DP, start_extra, 0)
    dp_extra[w.dp] = extra_ref[w.dp]
    for n in range(2):
        two[n, 2].relay()
    for k in range(4):
        pair[k].wait_recv()
        add_rows(WIDTH, 32, dense.at[2 * k + w.c], dense.at[2 * k + w.c], crossed.at[k])
    ring = RingSum(
        w, "x", lambda s: dense.at[w.at("x", s)], WIDTH, x_relayed, x_landed, x_send, x_recv, 0
    )
    ring.far()
    ring.near()
    for o in (1, -1, 0):
        for n in range(2):
            two[n, o].relay()
    ring.relay()
    for n in range(2):
        two[n, 2].finish(grads.at[n, w.at2(axes[n][0], 2, 0)])
        one[n].far()
    for n in range(2):
        for o in (1, -1):
            two[n, o].finish(grads.at[n, w.at2(axes[n][0], o, 0)])
        one[n].near()
    for n in range(2):
        one[n].relay()
        two[n, 0].finish(grads.at[n, w.dp])
    ring.finish(dense.at[w.e])

    def rows_of(dp):
        return pl.ds(pl.multiple_of(dp * ROWS, 16), ROWS)

    def dense_dp(k):
        peer = lax.rem(w.dp + k, DP)
        return remote(
            dense.at[w.e, rows_of(peer)],
            dp_got.at[w.dp],
            dp_send.at[0, k],
            dp_recv.at[0, k],
            {"dp": peer},
        )

    def start_dp(k, n):
        dense_dp(k).start()
        return n

    def end_dp(k, n):
        for copy in (dense_dp(k), extra_dp(k)):
            copy.wait_recv()
            copy.wait_send()
        return n

    lax.fori_loop(1, DP, start_dp, 0)
    dp_got[w.dp] = dense[w.e, rows_of(w.dp)]
    for n, ref in ((0, in_ref), (1, out_ref)):
        one[n].finish(ref)
    lax.fori_loop(1, DP, end_dp, 0)
    total = dp_got[0].astype(F32)
    extra_total = dp_extra[0]
    for k in range(1, DP):
        total = total + dp_got[k].astype(F32)
        extra_total = extra_total + dp_extra[k]
    extra_sum[...] = extra_total
    flat = jnp.concatenate([total[:, c * 128 : (c + 1) * 128] for c in range(3)], axis=0)
    last[...] = (
        jnp.dot(spread_ref[...], flat.astype(BF16), preferred_element_type=F32)
        .astype(BF16)
        .reshape(EXPERTS, 32, 128)
    )

    def to_expert(k):
        peer = lax.rem(w.e + k, EXPERTS)
        dev = {"expert": peer}
        return (
            remote(last.at[peer], last_got.at[w.e], a2a_send.at[0, k], a2a_recv.at[0, k], dev),
            remote(extra_sum, extra_got.at[w.e], a2a_send.at[1, k], a2a_recv.at[1, k], dev),
        )

    def start_a2a(k, n):
        for copy in to_expert(k):
            copy.start()
        return n

    def end_a2a(k, n):
        for copy in to_expert(k):
            copy.wait_recv()
            copy.wait_send()
        return n

    lax.fori_loop(1, EXPERTS, start_a2a, 0)
    last_got[w.e] = last[w.e]
    extra_got[w.e] = extra_sum[...]
    lax.fori_loop(1, EXPERTS, end_a2a, 0)
    dense_out_ref[...] = last_got[...].astype(F32)
    extra_total = extra_got[0]
    for k in range(1, EXPERTS):
        extra_total = extra_total + extra_got[k]
    extra_out_ref[...] = extra_total
    for copy in pair:
        copy.wait_send()
    ring.drain()
    for n in range(2):
        one[n].drain()
        for o in order:
            two[n, o].drain()


def reduce(gin, gout, dense, extra):
    hbm = pl.BlockSpec(memory_space=pl.ANY)
    vmem = pl.BlockSpec(memory_space=pltpu.VMEM)
    half = SHARD // 2
    return pl.pallas_call(
        reduce_kernel,
        out_shape=(
            jax.ShapeDtypeStruct((SHARD, WIDTH), F32),
            jax.ShapeDtypeStruct((SHARD, WIDTH), F32),
            jax.ShapeDtypeStruct((EXPERTS, 32, 128), F32),
            jax.ShapeDtypeStruct((16, 128), F32),
        ),
        in_specs=[hbm, hbm, hbm, vmem, vmem],
        out_specs=(vmem, vmem, vmem, vmem),
        scratch_shapes=[
            pltpu.VMEM((2, DP, SHARD, WIDTH), BF16),
            pltpu.VMEM((10, 2, half, WIDTH), BF16),
            pltpu.VMEM((10, 2, SHARD, WIDTH), BF16),
            pltpu.VMEM((EXPERTS, WIDTH, COLS), BF16),
            pltpu.VMEM((4, WIDTH, COLS), BF16),
            pltpu.VMEM((2, WIDTH // 2, COLS), BF16),
            pltpu.VMEM((2, WIDTH, COLS), BF16),
            pltpu.VMEM((DP, ROWS, COLS), BF16),
            pltpu.VMEM((DP, 16, 128), F32),
            pltpu.VMEM((16, 128), F32),
            pltpu.VMEM((EXPERTS, 32, 128), BF16),
            pltpu.VMEM((EXPERTS, 32, 128), BF16),
            pltpu.VMEM((EXPERTS, 16, 128), F32),
            pltpu.SemaphoreType.DMA((3,)),
            pltpu.SemaphoreType.DMA((60,)),
            pltpu.SemaphoreType.DMA((60,)),
            pltpu.SemaphoreType.DMA((10,)),
            pltpu.SemaphoreType.DMA((10,)),
            pltpu.SemaphoreType.DMA((2, DP)),
            pltpu.SemaphoreType.DMA((2, DP)),
            pltpu.SemaphoreType.DMA((2, EXPERTS)),
            pltpu.SemaphoreType.DMA((2, EXPERTS)),
        ],
        compiler_params=pltpu.CompilerParams(
            collective_id=1, has_side_effects=True, vmem_limit_bytes=56 * MIB
        ),
        name="reduce_gradients",
    )(gin, gout, dense, extra, jnp.asarray(spread_matrix(), BF16))


def contract_last(left, right):
    return lax.dot_general(left, right, (((1,), (1,)), ((), ())), preferred_element_type=F32)


def contract_first(left, right):
    return lax.dot_general(left, right, (((0,), (0,)), ((), ())), preferred_element_type=F32)


def local(
    tokens,
    w_qkv,
    w_attn_out,
    w_router,
    gain_attn,
    gain_moe,
    bias_table,
    w_in,
    w_out,
    expert_ids,
    slots,
    buckets,
    cotangent,
):
    seqs = tokens.shape[0] // LEN
    scale = HEAD_DIM ** (-0.5)
    me = lax.axis_index("expert")

    dense = jnp.concatenate([w_qkv, w_attn_out], axis=1)
    first = dense.reshape(6, EXPERTS, 3, 128).transpose(1, 2, 0, 3).reshape(EXPERTS, 18, 128)
    small = jnp.concatenate([w_router.reshape(48), gain_attn, gain_moe, bias_table])
    small = jnp.broadcast_to(jnp.pad(small, (0, 65))[None, None], (EXPERTS, 1, 128))
    first = jnp.concatenate(
        [first, jnp.zeros((EXPERTS, 14, 128), BF16), small, jnp.zeros((EXPERTS, 15, 128), BF16)],
        axis=1,
    )
    all_in, all_out, dense, extra = gather(w_in[0], w_out[0], first)
    all_in = all_in.reshape(FF, WIDTH)
    all_out = all_out.reshape(FF, WIDTH)
    wqkv = dense[:6].transpose(1, 0, 2).reshape(WIDTH, 3 * WIDTH)
    wattn = dense[6:].transpose(1, 0, 2).reshape(WIDTH, WIDTH)
    extra = extra[:, :8].reshape(128, 128).astype(F32)
    router = extra[:, :48].reshape(WIDTH, EXPERTS)
    gain_one = extra[:, 48:54].reshape(WIDTH)
    gain_two = extra[:, 54:60].reshape(WIDTH)
    table = extra[:, 60:63].reshape(BUCKETS, HEADS)

    levels = lax.broadcasted_iota(jnp.int32, (BUCKETS, LEN, LEN), 0)
    bucket_onehot = (levels == buckets[None]).astype(F32)
    full_bias = jnp.einsum("bij,bh->hij", bucket_onehot, table, precision=HIGH)

    x = tokens.astype(F32)
    rho1 = lax.rsqrt(jnp.mean(x * x, axis=-1, keepdims=True) + NORM_EPS)
    r1 = x * rho1
    n1 = (r1 * gain_one).astype(BF16)
    qkv = jnp.dot(n1, wqkv, preferred_element_type=F32).astype(BF16)
    heads = qkv.reshape(seqs, LEN, 3, HEADS, HEAD_DIM)
    q, k, v = heads[:, :, 0], heads[:, :, 1], heads[:, :, 2]
    s = jnp.einsum("sihc,sjhc->shij", q, k, preferred_element_type=F32) * scale + full_bias
    shifted = jnp.exp(s - jnp.max(s, axis=-1, keepdims=True))
    p = shifted / jnp.sum(shifted, axis=-1, keepdims=True)
    p_b = p.astype(BF16)
    attn = jnp.einsum("shij,sjhc->sihc", p_b, v, preferred_element_type=F32)
    attn = attn.reshape(seqs * LEN, WIDTH).astype(BF16)
    h1 = x + jnp.dot(attn, wattn, preferred_element_type=F32)
    rho2 = lax.rsqrt(jnp.mean(h1 * h1, axis=-1, keepdims=True) + NORM_EPS)
    r2 = h1 * rho2
    n2 = (r2 * gain_two).astype(BF16)
    n2f = n2.astype(F32)
    logits = jnp.dot(n2f, router, precision=HIGH)
    probs = jax.nn.softmax(logits, axis=-1)
    onehot = (
        expert_ids[:, None] == lax.broadcasted_iota(jnp.int32, (seqs * LEN, EXPERTS), 1)
    ).astype(F32)
    gate = jnp.sum(probs * onehot, axis=-1, keepdims=True)
    deo = (gate * cotangent).astype(BF16)

    target = expert_ids * CAP + slots
    columns = lax.broadcasted_iota(jnp.int32, (seqs * LEN, EXPERTS * CAP), 1)
    route = ((target[:, None] == columns) & (slots[:, None] < CAP)).astype(BF16)
    route = route.reshape(seqs, LEN, EXPERTS * CAP)
    both = jnp.stack([n2.reshape(seqs, LEN, WIDTH), deo.reshape(seqs, LEN, WIDTH)])
    sent = jnp.einsum("stc,kstd->kscd", route, both, preferred_element_type=F32).astype(BF16)
    sent = sent.reshape(2, seqs, EXPERTS, CAP, WIDTH).transpose(2, 0, 1, 3, 4)
    arrived = exchange(sent.reshape(EXPERTS, 2 * seqs * CAP, WIDTH), 2, "to_experts")
    arrived = arrived.reshape(EXPERTS, 2, seqs * CAP, WIDTH)
    rows = arrived[:, 0].reshape(EXPERTS * seqs * CAP, WIDTH)
    drows = arrived[:, 1].reshape(EXPERTS * seqs * CAP, WIDTH)

    pre = contract_last(rows, all_in)
    activated, gelu_back = jax.vjp(jax.nn.gelu, pre)
    hid = activated.astype(BF16)
    eo = jnp.dot(hid, all_out, preferred_element_type=F32).astype(BF16)
    dhid = contract_last(drows, all_out)
    dpre = gelu_back(dhid)[0].astype(BF16)
    dn2e = jnp.dot(dpre, all_in, preferred_element_type=F32).astype(BF16)
    gin = contract_first(dpre, rows).astype(BF16)
    gout = contract_first(hid, drows).astype(BF16)

    back = jnp.stack(
        [
            eo.reshape(EXPERTS, seqs * CAP, WIDTH),
            dn2e.reshape(EXPERTS, seqs * CAP, WIDTH),
        ],
        axis=1,
    )
    back = exchange(back.reshape(EXPERTS, 2 * seqs * CAP, WIDTH), 3, "from_experts")
    back = back.reshape(EXPERTS, 2, seqs, CAP, WIDTH).transpose(1, 2, 0, 3, 4)
    back = back.reshape(2, seqs, EXPERTS * CAP, WIDTH)
    combined = jnp.einsum("stc,kscd->kstd", route, back, preferred_element_type=F32)
    combined = combined.reshape(2, seqs * LEN, WIDTH)
    output = h1 + gate * combined[0]
    dgate = jnp.sum(cotangent * combined[0], axis=-1, keepdims=True)
    dlogits = probs * (onehot - gate) * dgate
    grad_router = lax.dot_general(n2f, dlogits, (((0,), (0,)), ((), ())), precision=HIGH)
    dn2 = lax.dot_general(dlogits, router, (((1,), (1,)), ((), ())), precision=HIGH) + combined[1]
    grad_gain_two = jnp.sum(dn2 * r2, axis=0)
    u2 = dn2 * gain_two
    dh1 = cotangent + rho2 * (u2 - r2 * jnp.mean(u2 * r2, axis=-1, keepdims=True))
    da = dh1.astype(BF16)
    grad_attn = contract_first(attn, da)
    dattn = contract_last(da, wattn).astype(BF16).reshape(seqs, LEN, HEADS, HEAD_DIM)
    dv = jnp.einsum("shij,sihc->sjhc", p_b, dattn, preferred_element_type=F32)
    dp = jnp.einsum("sihc,sjhc->shij", dattn, v, preferred_element_type=F32)
    ds = p * (dp - jnp.sum(p * dp, axis=-1, keepdims=True))
    grad_bias = jnp.einsum("bij,hij->bh", bucket_onehot, jnp.sum(ds, axis=0), precision=HIGH)
    ds_b = ds.astype(BF16)
    dq = jnp.einsum("shij,sjhc->sihc", ds_b, k, preferred_element_type=F32) * scale
    dk = jnp.einsum("shij,sihc->sjhc", ds_b, q, preferred_element_type=F32) * scale
    dqkv = jnp.stack([dq, dk, dv], axis=2).reshape(seqs * LEN, 3 * WIDTH).astype(BF16)
    grad_qkv = contract_first(n1, dqkv)
    dn1 = contract_last(dqkv, wqkv)
    grad_gain_one = jnp.sum(dn1 * r1, axis=0)
    u1 = dn1 * gain_one
    grad_tokens = dh1 + rho1 * (u1 - r1 * jnp.mean(u1 * r1, axis=-1, keepdims=True))

    dgrads = jnp.concatenate([grad_qkv, grad_attn], axis=1).astype(BF16)
    dgrads = dgrads.reshape(WIDTH, EXPERTS, COLS).transpose(1, 0, 2)
    small = jnp.concatenate(
        [
            grad_router.reshape(128, 48),
            grad_gain_one.reshape(128, 6),
            grad_gain_two.reshape(128, 6),
            grad_bias.reshape(128, 3),
            jnp.zeros((128, 65), F32),
        ],
        axis=1,
    ).reshape(DP, 8, 128)
    small = jnp.concatenate([small, jnp.zeros((DP, 8, 128), F32)], axis=1)
    grad_in, grad_out, dense_out, small = reduce(
        gin.reshape(DP, SHARD, WIDTH), gout.reshape(DP, SHARD, WIDTH), dgrads, small
    )
    dense_out = dense_out[:, :18].reshape(EXPERTS, 3, 6, 128).transpose(2, 0, 1, 3)
    dense_out = dense_out.reshape(6, EXPERTS * COLS)
    small = lax.dynamic_index_in_dim(small, me, 0, keepdims=False)
    return (
        output,
        grad_tokens,
        dense_out[:, : 3 * WIDTH],
        dense_out[:, 3 * WIDTH :],
        small[:48].reshape(6, EXPERTS),
        small[48:54],
        small[54:60],
        small[60:63],
        grad_in[None],
        grad_out[None],
    )


def solution(mesh):
    spread = ("dp", "expert")
    in_specs = (
        P(spread, None),
        P(spread, None),
        P(spread, None),
        P(spread, None),
        P(spread),
        P(spread),
        P(spread),
        P("expert", "dp", None),
        P("expert", "dp", None),
        P(spread),
        P(spread),
        P(),
        P(spread, None),
    )
    out_specs = (
        P(spread, None),
        P(spread, None),
        P(spread, None),
        P(spread, None),
        P(spread, None),
        P(spread),
        P(spread),
        P(spread),
        P("expert", "dp", None),
        P("expert", "dp", None),
    )
    return jax.shard_map(local, mesh=mesh, in_specs=in_specs, out_specs=out_specs, check_vma=False)
```

time: 1860 us -> 287 us (0.15)
  blocking collectives: 888 us -> 0 us
  waiting for transfers between devices: 462 us -> 0 us
  starting transfers between devices: 210 us -> 0 us
  Pallas kernels: 0 us -> 162 us
  matrix products: 124 us -> 47 us
  local copies, waits for them, and re-layouts: 99.3 us -> 61.6 us
  other arithmetic: 38.7 us -> 13.3 us
    unnamed x3 -> x0, blocking collectives: 495 us -> none
    all_gather x16 -> x0, waiting for transfers between devices: 430 us -> none  [the longest x2 112 us: expert_forward(): piece_in = lax.all_gather(w_in, 'dp', axis=1, tiled=True)]
    while x4 -> x0, blocking collectives: 258 us -> none
    unnamed x64 -> x0, starting transfers between devices: 174 us -> none
    pallas_call x0 -> x4, Pallas kernels: none -> 162 us  [the longest x1 70.2 us: reduce(): pl.pallas_call(reduce_kernel, out_shape=(jax.ShapeDtypeStruct((SHARD, WID...]
    all_gather x4 -> x0, blocking collectives: 136 us -> none  [the longest x2 68 us: forward_step(): lax.all_gather(w_router, ('dp', 'expert'), axis=0, tiled=True)]
    while x262 -> x0, local copies, waits for them, and re-layouts: 51 us -> none
    dot_general x12 -> x4, matrix products: 48.5 us -> 12.6 us  [contract_first(): lax.dot_general(left, right, (((0,), (0,)), ((), ())), preferred_element_...]
  transfers between devices with their start and end apart: 90 -> 0, of which waited for: 16 -> 0; matrix products, arithmetic and copies ran while one was open for 29% -> 0% of each run, Pallas kernels for 0% -> 0%
where the time goes in v1:
time: 287 us; the launch traced here: 286 us
  Pallas kernels  162 us (56%)
  local copies, waits for them, and re-layouts  61.6 us (21%)
  matrix products  47 us (16%)
  other arithmetic  13.3 us (5%)
    pallas_call x1, Pallas kernels, reduce(): pl.pallas_call(reduce_kernel, out_shape=(jax.ShapeDtypeStruct((SHARD, WID...  70.2 us
    pallas_call x1, Pallas kernels, gather(): pl.pallas_call(gather_kernel, out_shape=(jax.ShapeDtypeStruct((DP, SHARD,...  64.7 us
    pallas_call x2, Pallas kernels, exchange(): pl.pallas_call(exchange_kernel, out_shape=jax.ShapeDtypeStruct(blocks.sha...  27.5 us
    unnamed x120, local copies, waits for them, and re-layouts  14.9 us
    dot_general x4, matrix products, contract_first(): lax.dot_general(left, right, (((0,), (0,)), ((), ())), preferred_element_...  12.6 us
    dot_general x4, matrix products, contract_last(): lax.dot_general(left, right, (((1,), (1,)), ((), ())), preferred_element_...  10.9 us
    convert_element_type x1, local copies, waits for them, and re-layouts, local(): dgrads = jnp.concatenate([grad_qkv, grad_attn], axis=1).astype(BF16)  6.65 us
    concatenate x1, local copies, waits for them, and re-layouts, local(): dgrads = jnp.concatenate([grad_qkv, grad_attn], axis=1).astype(BF16)  6.62 us

profile of v1, /device:TPU:1, one launch (start us, length us, event | category | flops | bytes accessed | tf_op | source)
XLA Modules:
  0.0 285.7 jit_solution(13101514002269776272)
XLA Ops:
  6.2 64.7 %gather_weights.1 = (bf16[16,192,768]{2,1,0:T(8,128)(2,1)S(1)}, bf16[16,192,768]{2,1,0:T(8,128)(2,1)S(1)}, bf16[8,768,384]{2,1,0:T(8,128)(2,1)S(1)}, bf16[16,16,128]{2,1,0:T(8,128)(2,1)S(1)}) custom-call(bf16[192,768]{1,0:T(8,128)(2,1)S(1)} %bitcast.178, bf16[192,768]{1,0:T(8,128)(2,1)S(1)} %bitcast.179, ...), custom_call_target="tpu_custom_call" | custom-call | tf_op jit(solution)/shard_map/gather_weights/pallas_call | solution.py:301
  70.9 2.2 copy-done
  73.1 2.1 copy-done.1
  75.2 2.2 copy-done.5
  78.9 2.4 slice_bitcast_fusion
  81.3 3.7 %copy.113 = bf16[768,6,384]{0,2,1:T(8,128)(2,1)} copy(bf16[768,6,384]{2,0,1:T(8,128)(2,1)S(1)} %slice_bitcast_fusion) | data formatting | bytes 7077888 | tf_op jit(solution)/shard_map/transpose | solution.py:727
  86.7 3.3 %convolution_convert_fusion.3 = bf16[256,2304]{1,0:T(8,128)(2,1)S(1)} fusion(bf16[768,2304]{0,1:T(8,128)(2,1)} %bitcast.194, bf16[256,768]{1,0:T(8,128)(2,1)} %param.15, f32[768]{0:T(1024)S(1)} %mul.202, f32[256]{0:T(256)S(1)} %add_rsqrt_fusion.1), kind=kOutput, calls=%fused_computation.7 | convolution fusion | flops 907345920 | bytes 5115904 | tf_op jit(solution)/shard_map/dot_general | solution.py:743
  91.0 2.0 fusion.79
  109.7 14.6 %to_experts.1 = bf16[8,64,768]{2,1,0:T(8,128)(2,1)} custom-call(bf16[8,64,768]{2,1,0:T(8,128)(2,1)} %bitcast.199), custom_call_target="tpu_custom_call" | custom-call | tf_op jit(solution)/shard_map/to_experts/pallas_call | solution.py:359
  125.8 4.2 %fusion.84 = f32[256,3072]{1,0:T(8,128)S(1)} fusion(bf16[256,768]{1,0:T(8,128)(2,1)S(1)} %bitcast.205, bf16[3072,768]{1,0:T(8,128)(2,1)} %bitcast.174), kind=kOutput, calls=%fused_computation.143 | convolution fusion | flops 1207959552 | bytes 8257536 | tf_op jit(solution)/shard_map/dot_general | solution.py:690
  130.0 3.6 %fusion.7 = (bf16[256,3072]{1,0:T(8,128)(2,1)S(1)}, f32[256,3072]{1,0:T(8,128)S(1)}) fusion(f32[256,3072]{1,0:T(8,128)S(1)} %fusion.84, bf16[256,768]{1,0:T(8,128)(2,1)S(1)} %bitcast.203, bf16[3072,768]{1,0:T(8,128)(2,1)S(1)} %bitcast.182), kind=kOutput, calls=%fused_computation.15 | convolution fusion | flops 1223688192 | bytes 12976128 | tf_op jit(solution)/shard_map/dot_general | solution.py:690
  133.7 2.0 convolution_convert_fusion.8
  138.3 12.9 %from_experts.1 = bf16[8,64,768]{2,1,0:T(8,128)(2,1)} custom-call(bf16[8,64,768]{2,1,0:T(8,128)(2,1)} %bitcast.198), custom_call_target="tpu_custom_call" | custom-call | tf_op jit(solution)/shard_map/from_experts/pallas_call | solution.py:359
  157.7 2.3 multiply_reduce_fusion.1
  160.0 2.3 multiply_add_fusion.1
  163.3 2.0 multiply_reduce_fusion
  170.4 2.6 fusion.32
  179.2 1.9 convolution_convert_fusion
  181.7 2.8 pad_maximum_fusion
  184.4 6.6 %copy.138 = bf16[768,3072]{0,1:T(8,128)(2,1)} copy(bf16[768,3072]{1,0:T(8,128)(2,1)} %pad_maximum_fusion) | data formatting | bytes 9437184 | tf_op jit(solution)/shard_map/concatenate | solution.py:824
  191.1 6.6 %copy.139 = bf16[768,8,384]{2,0,1:T(8,128)(2,1)} copy(bf16[768,8,384]{0,2,1:T(8,128)(2,1)} %bitcast.186) | data formatting | bytes 9437184 | tf_op jit(solution)/shard_map/convert_element_type | solution.py:824
  197.7 6.5 %convolution_convert_fusion.1 = bf16[3072,768]{1,0:T(8,128)(2,1)} fusion(bf16[256,768]{1,0:T(8,128)(2,1)S(1)} %bitcast.206, f32[256,3072]{1,0:T(8,128)} %copy-done.54), kind=kOutput, calls=%fused_computation.2 | convolution fusion | flops 1217396736 | bytes 8257536 | tf_op jit(solution)/shard_map/dot_general | solution.py:694
  204.2 3.7 %convolution_convert_fusion.2 = bf16[3072,768]{1,0:T(8,128)(2,1)} fusion(bf16[256,3072]{1,0:T(8,128)(2,1)S(1)} %copy-done.14, bf16[256,768]{1,0:T(8,128)(2,1)S(1)} %bitcast.204), kind=kOutput, calls=%fused_computation.3 | convolution fusion | flops 1210318848 | bytes 6684672 | tf_op jit(solution)/shard_map/dot_general | solution.py:694
  207.9 70.2 %reduce_gradients.1 = (f32[192,768]{1,0:T(8,128)}, f32[192,768]{1,0:T(8,128)}, f32[8,32,128]{2,1,0:T(8,128)}, f32[16,128]{1,0:T(8,128)}) custom-call(bf16[16,192,768]{2,1,0:T(8,128)(2,1)} %bitcast.184, bf16[16,192,768]{2,1,0:T(8,128)(2,1)} %bitcast.189, bf16[8,768,384]{2,1,0:T(8,128)(2,1)} %bitcast.185, f32[16,16,128]{2,1,0:T(8,128)} %concatenate.37.extra_ref, ...), custom_call_target="tpu_custom_call" | custom-call | tf_op jit(solution)/shard_map/reduce_gradients/pallas_call | solution.py:648
  (201 shorter events, 56.8 us)
Async XLA Ops:
  78.9 90.8 %copy-start.35 = (f32[768]{0:T(1024)}, f32[768]{0:T(1024)S(1)}, u32[]{:S(2)}) copy-start(f32[768]{0:T(1024)S(1)} %mul.202) | copy-start | bytes 9220
  101.3 5.8 %copy-start.6 = (f32[256,768]{1,0:T(8,128)S(1)}, f32[256,768]{1,0:T(8,128)}, u32[]{:S(2)}) copy-start(f32[256,768]{1,0:T(8,128)} %param.27) | copy-start | bytes 2359300
  102.0 5.1 %copy-start.43 = (s32[256]{0:T(256)S(1)}, s32[256]{0:T(256)}, u32[]{:S(2)}) copy-start(s32[256]{0:T(256)} %param.24) | copy-start | bytes 3076
  102.0 5.3 %copy-start.52 = (s32[256]{0:T(256)S(1)}, s32[256]{0:T(256)}, u32[]{:S(2)}) copy-start(s32[256]{0:T(256)} %param.25) | copy-start | bytes 3076
  105.5 24.5 %slice-start.2 = ((s8[4718592]{0:T(1024)(128)(4,1)}), s8[524288]{0:T(1024)(128)(4,1)S(1)}, s32[]{:S(2)}) async-start(s8[4718592]{0:T(1024)(128)(4,1)} %bitcast.180), calls=%async_computation.2 | async-start | bytes 1048576
  105.6 18.7 %copy-start.15 = (bf16[768,8]{1,0:T(8,128)(2,1)}, bf16[768,8]{1,0:T(8,128)(2,1)S(1)}, u32[]{:S(2)}) copy-start(bf16[768,8]{1,0:T(8,128)(2,1)S(1)} %reshape.190) | copy-start | bytes 36868
  107.0 18.7 %copy-start.37 = (f32[256]{0:T(256)}, f32[256]{0:T(256)S(1)}, u32[]{:S(2)}) copy-start(f32[256]{0:T(256)S(1)} %get-tuple-element.51) | copy-start | bytes 3076
  107.0 18.7 %copy-start.45 = (f32[256]{0:T(256)}, f32[256]{0:T(256)S(1)}, u32[]{:S(2)}) copy-start(f32[256]{0:T(256)S(1)} %fusion.64) | copy-start | bytes 3076
  107.1 18.6 %copy-start.39 = (f32[256]{0:T(256)}, f32[256]{0:T(256)S(1)}, u32[]{:S(2)}) copy-start(f32[256]{0:T(256)S(1)} %select_reduce_fusion) | copy-start | bytes 3076
  124.4 5.6 %slice-start.3 = ((s8[4718592]{0:T(1024)(128)(4,1)}), s8[4194304]{0:T(1024)(128)(4,1)S(1)}, s32[]{:S(2)}) async-start(s8[4718592]{0:T(1024)(128)(4,1)} %bitcast.180), calls=%async_computation.3 | async-start | bytes 8388608
  125.7 4.2 %copy-start.18 = (bf16[8,1,32,768]{3,2,1,0:T(8,128)(2,1)}, bf16[8,1,32,768]{3,2,1,0:T(8,128)(2,1)S(1)}, u32[]{:S(2)}) copy-start(bf16[8,1,32,768]{3,2,1,0:T(8,128)(2,1)S(1)} %get-tuple-element.39) | copy-start | bytes 1179652
  125.8 7.9 %slice-start = ((s8[4718592]{0:T(1024)(128)(4,1)}), s8[4194304]{0:T(1024)(128)(4,1)S(1)}, s32[]{:S(2)}) async-start(s8[4718592]{0:T(1024)(128)(4,1)} %bitcast.175), calls=%async_computation | async-start | bytes 8388608
  170.4 5.0 %copy-start.33 = (s32[128,128]{1,0:T(8,128)S(1)}, s32[128,128]{1,0:T(8,128)}, u32[]{:S(2)}) copy-start(s32[128,128]{1,0:T(8,128)} %param.26) | copy-start | bytes 196612
  173.0 4.6 %copy-start.34 = (f32[16,8,48]{2,1,0:T(8,128)S(1)}, f32[16,8,48]{2,1,0:T(8,128)}, u32[]{:S(2)}) copy-start(f32[16,8,48]{2,1,0:T(8,128)} %concatenate.32) | copy-start | bytes 73732
  176.6 4.6 %copy-start.10 = (bf16[2,128,12,64]{1,0,3,2:T(2,128)(2,1)S(1)}, bf16[2,128,12,64]{1,0,3,2:T(2,128)(2,1)}, u32[]{:S(2)}) copy-start(bf16[2,128,12,64]{1,0,3,2:T(2,128)(2,1)} %copy.121) | copy-start | bytes 1179652
  191.1 6.7 %copy-start.19 = (bf16[8,1,32,768]{3,2,1,0:T(8,128)(2,1)S(1)}, bf16[8,1,32,768]{3,2,1,0:T(8,128)(2,1)}, u32[]{:S(2)}) copy-start(bf16[8,1,32,768]{3,2,1,0:T(8,128)(2,1)} %copy-done.18) | copy-start | bytes 1179652
  197.7 6.5 %copy-start.14 = (bf16[256,3072]{1,0:T(8,128)(2,1)S(1)}, bf16[256,3072]{1,0:T(8,128)(2,1)}, u32[]{:S(2)}) copy-start(bf16[256,3072]{1,0:T(8,128)(2,1)} %copy-done.13) | copy-start | bytes 4718596
  197.7 6.5 %copy-start.17 = (bf16[8,1,32,768]{3,2,1,0:T(8,128)(2,1)S(1)}, bf16[8,1,32,768]{3,2,1,0:T(8,128)(2,1)}, u32[]{:S(2)}) copy-start(bf16[8,1,32,768]{3,2,1,0:T(8,128)(2,1)} %copy-done.16) | copy-start | bytes 1179652
  207.9 75.1 %copy-start.53 = (f32[256]{0:T(256)S(1)}, f32[256]{0:T(256)}, u32[]{:S(2)}) copy-start(f32[256]{0:T(256)} %get-tuple-element.29) | copy-start | bytes 3076
  207.9 75.1 %copy-start.26 = (f32[256,768]{1,0:T(8,128)S(1)}, f32[256,768]{1,0:T(8,128)}, u32[]{:S(2)}) copy-start(f32[256,768]{1,0:T(8,128)} %get-tuple-element.58) | copy-start | bytes 2359300
  207.9 75.1 %copy-start.36 = (f32[768]{0:T(1024)S(1)}, f32[768]{0:T(1024)}, u32[]{:S(2)}) copy-start(f32[768]{0:T(1024)} %copy-done.35) | copy-start | bytes 9220
  207.9 75.1 %copy-start.50 = (f32[256]{0:T(256)S(1)}, f32[256]{0:T(256)}, u32[]{:S(2)}) copy-start(f32[256]{0:T(256)} %copy-done.48) | copy-start | bytes 3076
  278.0 6.1 %copy-start.28 = (f32[192,768]{1,0:T(8,128)S(1)}, f32[192,768]{1,0:T(8,128)}, u32[]{:S(2)}) copy-start(f32[192,768]{1,0:T(8,128)} %get-tuple-element.24) | copy-start | bytes 1769476
  278.0 6.9 %copy-start.27 = (f32[192,768]{1,0:T(8,128)S(1)}, f32[192,768]{1,0:T(8,128)}, u32[]{:S(2)}) copy-start(f32[192,768]{1,0:T(8,128)} %get-tuple-element.25) | copy-start | bytes 1769476
  (35 other events, 73.3 us)

commit v2 on v1

v2 whole, which is shorter than its diff:
```python
import math

import jax
import jax.numpy as jnp
import numpy as np
from jax import lax
from jax.experimental import pallas as pl
from jax.experimental.pallas import tpu as pltpu
from jax.sharding import PartitionSpec as P

MESH = pl.DeviceIdType.MESH
HEADS = 12
HEAD_DIM = 64
BUCKETS = 32
LEN = 128
WIDTH = 768
FF = 3072
EXPERTS = 8
DP = 16
CAP = 16
SHARD = FF // DP
COLS = 384
ROWS = 48
NORM_EPS = 1e-06
HIGH = lax.Precision.HIGHEST
F32 = jnp.float32
BF16 = jnp.bfloat16
MIB = 1 << 20


def place_matrix():
    m = np.zeros((160, 384), np.float32)
    for c in range(3):
        for e in range(8):
            for r in range(6):
                m[c * 48 + e * 6 + r, e * 48 + c * 6 + r] = 1
    for e in range(8):
        m[144 + e, e * 48 + 32] = 1
    return m


def spread_matrix():
    m = np.zeros((256, 144), np.float32)
    for c in range(3):
        for e in range(8):
            for r in range(6):
                m[e * 32 + c * 6 + r, c * 48 + e * 6 + r] = 1
    return m


def small_matrices():
    n = np.arange(WIDTH)
    owner = np.zeros((128, WIDTH), np.float32)
    owner[n // 6, n] = 1
    gains = np.zeros((2, 128, WIDTH), np.float32)
    gains[0, 48 + n % 6, n] = 1
    gains[1, 56 + n % 6, n] = 1
    col = np.arange(128)
    group = ((col[None] // 8 == n[:, None] % 6) & (col[None] < 48)).astype(np.float32)
    fold = np.zeros((128, 128), np.float32)
    fold[np.arange(48), np.arange(48) % 8] = 1
    table = np.zeros((128, 128), np.float32)
    for j in range(4):
        for b in range(BUCKETS):
            table[4 * b + j, j * 32 + b] = 1
    pick = np.zeros((4, 16, 128), np.float32)
    for j in range(4):
        for t in range(3):
            pick[j, 3 * j + t, 64 + t] = 1
    return owner, gains, group, fold, table, pick


class Where:
    def __init__(self):
        self.dp = lax.axis_index("dp")
        self.e = lax.axis_index("expert")
        self.z, self.y = lax.div(self.dp, 4), lax.rem(self.dp, 4)
        self.x, self.c = lax.div(self.e, 2), lax.rem(self.e, 2)
        self.partner_e = self.x * 2 + (1 - self.c)
        self.partner = {"expert": self.partner_e}

    def at(self, axis, step):
        if axis == "y":
            return self.z * 4 + lax.rem(self.y + step + 4, 4)
        if axis == "z":
            return lax.rem(self.z + step + 4, 4) * 4 + self.y
        return lax.rem(self.x + step + 4, 4) * 2 + self.c

    def dev(self, axis, step):
        return {"expert" if axis == "x" else "dp": self.at(axis, step)}

    def at2(self, axis1, step1, step2):
        dy, dz = (step1, step2) if axis1 == "y" else (step2, step1)
        return lax.rem(self.z + dz + 4, 4) * 4 + lax.rem(self.y + dy + 4, 4)


def greet(w, dp_too):
    barrier = pltpu.get_barrier_semaphore()

    def hello_e(k, n):
        pl.semaphore_signal(
            barrier, inc=1, device_id={"expert": lax.rem(w.e + k, EXPERTS)}, device_id_type=MESH
        )
        return n

    def hello_dp(k, n):
        pl.semaphore_signal(
            barrier, inc=1, device_id={"dp": lax.rem(w.dp + k, DP)}, device_id_type=MESH
        )
        return n

    lax.fori_loop(1, EXPERTS, hello_e, 0)
    if dp_too:
        lax.fori_loop(1, DP, hello_dp, 0)
    pl.semaphore_wait(barrier, EXPERTS - 1 + (DP - 1 if dp_too else 0))


def remote(src, dst, send, recv, dev):
    return pltpu.make_async_remote_copy(
        src_ref=src, dst_ref=dst, send_sem=send, recv_sem=recv, device_id=dev, device_id_type=MESH
    )


class RingGather:
    def __init__(self, w, axis, place, rows, send, recv, base, own=None):
        self.w, self.axis, self.place, self.half = w, axis, place, rows // 2
        self.send, self.recv, self.base = send, recv, base
        self.own = place(0) if own is None else own
        self.copies = []

    def _go(self, k, src, dst, step):
        copy = remote(
            src,
            dst,
            self.send.at[self.base + k],
            self.recv.at[self.base + k],
            self.w.dev(self.axis, step),
        )
        copy.start()
        self.copies.append(copy)

    def start(self):
        self._go(0, self.own, self.place(0), 1)
        self._go(1, self.own, self.place(0), -1)

    def relay(self):
        h = self.half
        self.copies[0].wait_recv()
        low = self.place(-1).at[pl.ds(0, h)]
        self._go(2, low, low, 1)
        self.copies[1].wait_recv()
        high = self.place(1).at[pl.ds(h, h)]
        self._go(3, high, high, -1)

    def finish(self):
        self.copies[2].wait_recv()
        self.copies[3].wait_recv()

    def drain(self):
        for copy in self.copies:
            copy.wait_send()


def add_rows(rows, step, dst, *srcs):
    def body(i, n):
        part = pl.ds(pl.multiple_of(i * step, step), step)
        total = srcs[0][part].astype(F32)
        for src in srcs[1:]:
            total = total + src[part].astype(F32)
        dst[part] = total.astype(dst.dtype)
        return n

    lax.fori_loop(0, rows // step, body, 0)


class RingSum:
    def __init__(self, w, axis, place, rows, relayed, landed, send, recv, base):
        self.w, self.axis, self.place, self.rows, self.half = w, axis, place, rows, rows // 2
        self.relayed, self.landed = relayed, landed
        self.send, self.recv, self.base = send, recv, base
        self.copies = {}

    def _go(self, k, src, dst, step):
        copy = remote(
            src,
            dst,
            self.send.at[self.base + k],
            self.recv.at[self.base + k],
            self.w.dev(self.axis, step),
        )
        copy.start()
        self.copies[k] = copy

    def _part(self, ref, k):
        return ref.at[pl.ds(k * self.half, self.half)]

    def far(self):
        self._go(0, self._part(self.place(2), 0), self.relayed.at[0], 1)
        self._go(1, self._part(self.place(2), 1), self.relayed.at[1], -1)

    def near(self):
        self._go(2, self._part(self.place(1), 1), self._part(self.landed.at[0], 1), 1)
        self._go(3, self._part(self.place(-1), 0), self._part(self.landed.at[1], 0), -1)

    def relay(self):
        self.copies[0].wait_recv()
        low = self._part(self.place(1), 0)
        add_rows(self.half, 32, low, low, self.relayed.at[0])
        self._go(4, low, self._part(self.landed.at[0], 0), 1)
        self.copies[1].wait_recv()
        high = self._part(self.place(-1), 1)
        add_rows(self.half, 32, high, high, self.relayed.at[1])
        self._go(5, high, self._part(self.landed.at[1], 1), -1)

    def finish(self, dst):
        for k in (2, 3, 4, 5):
            self.copies[k].wait_recv()
        add_rows(self.rows, 32, dst, self.place(0), self.landed.at[0], self.landed.at[1])

    def drain(self):
        for k in range(6):
            self.copies[k].wait_send()


def contract_last(left, right):
    return lax.dot_general(left, right, (((1,), (1,)), ((), ())), preferred_element_type=F32)


def contract_first(left, right):
    return lax.dot_general(left, right, (((0,), (0,)), ((), ())), preferred_element_type=F32)


def gelu_both(v):
    c = math.sqrt(2.0 / math.pi)
    square = v * v
    t = jnp.tanh(c * v * (1.0 + 0.044715 * square))
    half = 0.5 * (1.0 + t)
    slope = half + 0.5 * v * (1.0 - t * t) * (c * (1.0 + (3.0 * 0.044715) * square))
    return v * half, slope


def exact_dot(left, right):
    return jnp.dot(left, right, precision=HIGH, preferred_element_type=F32)


def layer_kernel(
    x_ref,
    cot_ref,
    ids_ref,
    slots_ref,
    buckets_ref,
    first_ref,
    place_ref,
    spread_ref,
    owner_ref,
    gains_ref,
    group_ref,
    fold_ref,
    table_ref,
    pick_ref,
    win_ref,
    wout_ref,
    output_ref,
    grad_tokens_ref,
    in_ref,
    out_ref,
    dense_out_ref,
    extra_out_ref,
    weights,
    dense,
    extra,
    got,
    piece,
    extra_piece,
    qkv,
    attn,
    n1,
    n2,
    h1,
    probs,
    gate,
    p_all,
    bias,
    router,
    gain,
    sent,
    arrived,
    back,
    returned,
    eo,
    dn2e,
    grads,
    relayed,
    landed,
    ddense,
    crossed,
    x_relayed,
    x_landed,
    dp_got,
    dp_extra,
    extra_mine,
    extra_sum,
    last,
    last_got,
    extra_got,
    da,
    dattn,
    dqkv,
    ds_sum,
    dlogits,
    gain_grads,
    bias_rows,
    own_sem,
    a2a_send,
    a2a_recv,
    dp_send,
    dp_recv,
    ring_send,
    ring_recv,
    x_send,
    x_recv,
    tok_send,
    tok_recv,
    sum_send,
    sum_recv,
    sx_send,
    sx_recv,
    sdp_send,
    sdp_recv,
    sa_send,
    sa_recv,
):
    w = Where()
    scale = HEAD_DIM ** (-0.5)
    greet(w, True)

    def to_expert(k):
        peer = lax.rem(w.e + k, EXPERTS)
        return remote(
            first_ref.at[peer], got.at[w.e], a2a_send.at[k], a2a_recv.at[k], {"expert": peer}
        )

    def start_a2a(k, n):
        to_expert(k).start()
        return n

    lax.fori_loop(1, EXPERTS, start_a2a, 0)
    got[w.e] = first_ref[w.e]
    owns = []
    one, two = {}, {}
    for n, (own, axis1, axis2) in enumerate(((win_ref, "y", "z"), (wout_ref, "z", "y"))):
        keep = pltpu.make_async_copy(own, weights.at[n, w.dp], own_sem.at[n])
        keep.start()
        owns.append(keep)
        one[n] = RingGather(
            w,
            axis1,
            lambda s, n=n, a=axis1: weights.at[n, w.at2(a, s, 0)],
            SHARD,
            ring_send,
            ring_recv,
            n * 20,
            own=own,
        )
        for k, o in enumerate((0, -1, 1, 2)):
            two[n, o] = RingGather(
                w,
                axis2,
                lambda s, n=n, a=axis1, o=o: weights.at[n, w.at2(a, o, s)],
                SHARD,
                ring_send,
                ring_recv,
                n * 20 + 4 + 4 * k,
                own=own if o == 0 else None,
            )
    for n in range(2):
        one[n].start()

    def end_a2a(k, n):
        copy = to_expert(k)
        copy.wait_recv()
        copy.wait_send()
        return n

    lax.fori_loop(1, EXPERTS, end_a2a, 0)
    placed = jnp.dot(place_ref[...], got[...].reshape(384, 128), preferred_element_type=F32).astype(
        BF16
    )
    for c in range(3):
        piece[:, c * 128 : (c + 1) * 128] = placed[c * 48 : (c + 1) * 48]
    extra_piece[...] = placed[144:160]
    mine = pl.ds(pl.multiple_of(w.dp * ROWS, 16), ROWS)

    def to_dp(k):
        dev = {"dp": lax.rem(w.dp + k, DP)}
        return (
            remote(piece, dense.at[w.e, mine], dp_send.at[0, k], dp_recv.at[0, k], dev),
            remote(extra_piece, extra.at[w.dp], dp_send.at[1, k], dp_recv.at[1, k], dev),
        )

    def start_dp(k, n):
        for copy in to_dp(k):
            copy.start()
        return n

    def end_dp(k, n):
        for copy in to_dp(k):
            copy.wait_recv()
            copy.wait_send()
        return n

    lax.fori_loop(1, DP, start_dp, 0)
    dense[w.e, mine] = piece[...]
    extra[w.dp] = extra_piece[...]
    for n in range(2):
        two[n, 0].start()
    x = x_ref[...].astype(F32)
    rho1 = lax.rsqrt(jnp.mean(x * x, axis=-1, keepdims=True) + NORM_EPS)
    lax.fori_loop(1, DP, end_dp, 0)
    ring = RingGather(w, "x", lambda s: dense.at[w.at("x", s)], WIDTH, x_send, x_recv, 0)
    ring.start()

    def across(k, ref):
        copy = remote(ref, ref, x_send.at[4 + k], x_recv.at[4 + k], w.partner)
        copy.start()
        return copy

    pair = [across(0, dense.at[w.e])]
    for n in range(2):
        one[n].relay()
        two[n, -1].start()
        two[n, 1].start()

    small = extra[...].astype(F32)[:, :8].reshape(128, 128).astype(BF16)
    owner = owner_ref[...]
    for n in range(2):
        tiled = jnp.dot(small, gains_ref[n], preferred_element_type=F32)
        gain[n : n + 1] = jnp.sum(tiled * owner.astype(F32), axis=0, keepdims=True)
    rows_small = contract_first(owner, small) * group_ref[...].astype(F32)
    router[...] = jnp.dot(
        rows_small.astype(BF16), fold_ref[...], preferred_element_type=F32
    ).astype(BF16)
    tables = contract_first(small, table_ref[...])
    buckets = buckets_ref[...]
    for h in range(HEADS):
        row = tables[64 + h % 3 : 65 + h % 3]
        bias[h] = jnp.take_along_axis(
            jnp.broadcast_to(row, (LEN, 128)), buckets + 32 * (h // 3), axis=1
        )
    n1[...] = (x * rho1 * gain[0:1]).astype(BF16)

    ring.relay()
    pair.append(across(1, dense.at[w.at("x", -1)]))
    pair.append(across(2, dense.at[w.at("x", 1)]))
    for n in range(2):
        two[n, 0].relay()
    for n in range(2):
        one[n].finish()
        two[n, 2].start()
    ring.finish()
    pair.append(across(3, dense.at[w.at("x", 2)]))
    for copy in pair:
        copy.wait_recv()
    for e in range(6):
        qkv[:, e * COLS : (e + 1) * COLS] = jnp.dot(
            n1[...], dense[e], preferred_element_type=F32
        ).astype(BF16)

    low_lanes = lax.broadcasted_iota(jnp.int32, (LEN, 128), 1) < HEAD_DIM
    lanes_of = (low_lanes, jnp.logical_not(low_lanes))
    zero = jnp.zeros((LEN, 128), BF16)

    def lanes_at(block, hp):
        return pl.ds(pl.multiple_of(block * WIDTH + hp * 128, 128), 128)

    def attention(s, lo, hi):
        rows = pl.ds(s * LEN, LEN)

        def pairs(i, n):
            for u in range(2):
                hp = 2 * i + u
                q, k, v = (qkv[rows, lanes_at(b, hp)] for b in range(3))
                outs = []
                for t in range(2):
                    h = 2 * hp + t
                    logit = contract_last(jnp.where(lanes_of[t], q, zero), k) * scale + bias[h]
                    shifted = jnp.exp(logit - jnp.max(logit, axis=-1, keepdims=True))
                    p = shifted / jnp.sum(shifted, axis=-1, keepdims=True)
                    p_all[s * HEADS + h] = p
                    outs.append(jnp.dot(p.astype(BF16), v, preferred_element_type=F32))
                attn[rows, lanes_at(0, hp)] = jnp.where(low_lanes, outs[0], outs[1]).astype(BF16)
            return n

        lax.fori_loop(lo, hi, pairs, 0)

    expert_lane = lax.broadcasted_iota(jnp.int32, (LEN, 128), 1)
    expert_row = lax.broadcasted_iota(jnp.int32, (LEN, 128), 0)
    eye16 = (
        lax.broadcasted_iota(jnp.int32, (16, 128), 0) == lax.broadcasted_iota(jnp.int32, (16, 128), 1)
    ).astype(BF16)

    def routing(s):
        ids, slots = ids_ref[s : s + 1], slots_ref[s : s + 1]
        target = jnp.where(slots < CAP, ids * CAP + slots, -1)
        route = (jnp.broadcast_to(target, (LEN, 128)) == expert_row).astype(F32).astype(BF16)
        hot_t = (
            (jnp.broadcast_to(ids, (16, LEN)) == lax.broadcasted_iota(jnp.int32, (16, LEN), 0))
            .astype(F32)
            .astype(BF16)
        )
        return route, contract_first(hot_t, eye16)

    def second_norm(s):
        rows = pl.ds(s * LEN, LEN)
        for e in range(2):
            cols = pl.ds(e * COLS, COLS)
            h1[rows, cols] = x_ref[rows, cols].astype(F32) + jnp.dot(
                attn[rows], dense[6 + e], preferred_element_type=F32
            )
        h = h1[rows]
        rho2 = lax.rsqrt(jnp.mean(h * h, axis=-1, keepdims=True) + NORM_EPS)
        normed = (h * rho2 * gain[1:2]).astype(BF16)
        n2[rows] = normed
        logits = jnp.dot(normed, router[...], preferred_element_type=F32)
        logits = jnp.where(expert_lane < EXPERTS, logits, -1e30)
        raised = jnp.exp(logits - jnp.max(logits, axis=-1, keepdims=True))
        prob = raised / jnp.sum(raised, axis=-1, keepdims=True)
        route, hot = routing(s)
        g = jnp.sum(prob * hot, axis=-1, keepdims=True)
        probs[rows] = prob
        gate[rows] = jnp.broadcast_to(g, (LEN, 128))
        deo = (g * cot_ref[rows]).astype(BF16)
        for kind, value in enumerate((normed, deo)):
            picked = jnp.dot(route, value, preferred_element_type=F32).astype(BF16)
            for e in range(EXPERTS):
                sent[s, e, kind] = picked[e * CAP : (e + 1) * CAP]

    def token_copy(src, dst, base, s, k):
        peer = lax.rem(w.e + k, EXPERTS)
        at = base + s * EXPERTS + k
        return remote(
            src.at[s, peer], dst.at[s, w.e], tok_send.at[at], tok_recv.at[at], {"expert": peer}
        )

    def send_tokens(src, dst, base, s):
        def begin(k, n):
            token_copy(src, dst, base, s, k).start()
            return n

        lax.fori_loop(1, EXPERTS, begin, 0)
        dst[s, w.e] = src[s, w.e]

    def wait_tokens(src, dst, base, s):
        def end(k, n):
            copy = token_copy(src, dst, base, s, k)
            copy.wait_recv()
            copy.wait_send()
            return n

        lax.fori_loop(1, EXPERTS, end, 0)

    attention(0, 0, 3)
    second_norm(0)
    send_tokens(sent, arrived, 0, 0)
    for n in range(2):
        two[n, -1].relay()
        two[n, 1].relay()
    attention(1, 0, 3)
    second_norm(1)
    send_tokens(sent, arrived, 0, 1)
    for n in range(2):
        two[n, 2].relay()
    for n in range(2):
        for o in (0, -1, 1, 2):
            two[n, o].finish()
    for s in range(2):
        wait_tokens(sent, arrived, 0, s)
    for copy in owns:
        copy.wait()

    slots_here = 2 * EXPERTS * CAP
    eo[...] = jnp.zeros_like(eo)
    dn2e[...] = jnp.zeros_like(dn2e)

    def hidden_block(j, n):
        block = pl.ds(2 * j, 2)
        w_in = weights[0, block].reshape(2 * SHARD, WIDTH)
        w_out = weights[1, block].reshape(2 * SHARD, WIDTH)
        rows = arrived[:, :, 0].reshape(slots_here, WIDTH)
        drows = arrived[:, :, 1].reshape(slots_here, WIDTH)
        act, slope = gelu_both(contract_last(rows, w_in))
        hid = act.astype(BF16)
        dpre = (contract_last(drows, w_out) * slope).astype(BF16)
        eo[...] += jnp.dot(hid, w_out, preferred_element_type=F32)
        dn2e[...] += jnp.dot(dpre, w_in, preferred_element_type=F32)
        grads[0, block] = contract_first(dpre, rows).astype(BF16).reshape(2, SHARD, WIDTH)
        grads[1, block] = contract_first(hid, drows).astype(BF16).reshape(2, SHARD, WIDTH)
        return n

    lax.fori_loop(0, DP // 2, hidden_block, 0)
    for s in range(2):
        for e in range(EXPERTS):
            rows = pl.ds((s * EXPERTS + e) * CAP, CAP)
            back[s, e, 0] = eo[rows].astype(BF16)
            back[s, e, 1] = dn2e[rows].astype(BF16)
        send_tokens(back, returned, 16, s)

    axes = (("y", "z"), ("z", "y"))
    order = (2, 1, -1, 0)
    sum1, sum2 = {}, {}
    for n, (axis1, axis2) in enumerate(axes):
        for k, o in enumerate(order):
            sum2[n, o] = RingSum(
                w,
                axis2,
                lambda s, n=n, a=axis1, o=o: grads.at[n, w.at2(a, o, s)],
                SHARD,
                relayed.at[n * 5 + k],
                landed.at[n * 5 + k],
                sum_send,
                sum_recv,
                (n * 5 + k) * 6,
            )
        sum1[n] = RingSum(
            w,
            axis1,
            lambda s, n=n, a=axis1: grads.at[n, w.at2(a, s, 0)],
            SHARD,
            relayed.at[n * 5 + 4],
            landed.at[n * 5 + 4],
            sum_send,
            sum_recv,
            (n * 5 + 4) * 6,
        )
    for o in order:
        for n in range(2):
            sum2[n, o].far()
    for o in order:
        for n in range(2):
            sum2[n, o].near()
    for n in range(2):
        sum2[n, 2].relay()

    gain_grads[...] = jnp.zeros_like(gain_grads)

    def second_norm_back(s):
        rows = pl.ds(s * LEN, LEN)
        route, hot = routing(s)
        combined = contract_first(route, returned[s, :, 0].reshape(LEN, WIDTH))
        g, cot, h = gate[rows, 0:1], cot_ref[rows], h1[rows]
        output_ref[rows] = h + g * combined
        dgate = jnp.sum(cot * combined, axis=-1, keepdims=True)
        dl = (probs[rows] * (hot - g) * dgate).astype(BF16)
        dlogits[rows] = dl
        dn2 = contract_last(dl, router[...]) + contract_first(
            route, returned[s, :, 1].reshape(LEN, WIDTH)
        )
        rho2 = lax.rsqrt(jnp.mean(h * h, axis=-1, keepdims=True) + NORM_EPS)
        r2 = h * rho2
        gain_grads[1:2] += jnp.sum(dn2 * r2, axis=0, keepdims=True)
        u2 = dn2 * gain[1:2]
        dh1 = cot + rho2 * (u2 - r2 * jnp.mean(u2 * r2, axis=-1, keepdims=True))
        h1[rows] = dh1
        da[rows] = dh1.astype(BF16)
        total = contract_last(da[rows, 0:COLS], dense[6])
        dattn[rows] = (total + contract_last(da[rows, COLS:WIDTH], dense[7])).astype(BF16)

    def attention_back(s, lo, hi):
        rows = pl.ds(s * LEN, LEN)

        def pairs(i, n):
            for u in range(2):
                hp = 2 * i + u
                q, k, v = (qkv[rows, lanes_at(b, hp)] for b in range(3))
                d_out = dattn[rows, lanes_at(0, hp)]
                dqs, dks, dvs = [], [], []
                for t in range(2):
                    h = 2 * hp + t
                    p = p_all[s * HEADS + h]
                    dprob = contract_last(jnp.where(lanes_of[t], d_out, zero), v)
                    ds = p * (dprob - jnp.sum(p * dprob, axis=-1, keepdims=True))
                    if s == 1:
                        ds_sum[h] = ds
                    else:
                        ds_sum[h] += ds
                    ds_b = ds.astype(BF16)
                    dvs.append(contract_first(p.astype(BF16), d_out))
                    dqs.append(jnp.dot(ds_b, k, preferred_element_type=F32))
                    dks.append(contract_first(ds_b, q))
                dqkv[rows, lanes_at(0, hp)] = (
                    jnp.where(low_lanes, dqs[0], dqs[1]) * scale
                ).astype(BF16)
                dqkv[rows, lanes_at(1, hp)] = (
                    jnp.where(low_lanes, dks[0], dks[1]) * scale
                ).astype(BF16)
                dqkv[rows, lanes_at(2, hp)] = jnp.where(low_lanes, dvs[0], dvs[1]).astype(BF16)
            return n

        lax.fori_loop(lo, hi, pairs, 0)

    wait_tokens(back, returned, 16, 1)
    second_norm_back(1)
    attention_back(1, 0, 3)
    for o in (1, -1):
        for n in range(2):
            sum2[n, o].relay()
    wait_tokens(back, returned, 16, 0)
    second_norm_back(0)
    for e in range(2):
        ddense[6 + e] = contract_first(attn[...], da[:, e * COLS : (e + 1) * COLS]).astype(BF16)
    for n in range(2):
        sum2[n, 0].relay()
    attention_back(0, 0, 3)
    for n in range(2):
        sum2[n, 2].finish(grads.at[n, w.at2(axes[n][0], 2, 0)])
        sum1[n].far()
    for e in range(6):
        ddense[e] = contract_first(n1[...], dqkv[:, e * COLS : (e + 1) * COLS]).astype(BF16)

    pair_sum = []
    for k in range(4):
        copy = remote(
            ddense.at[2 * k + 1 - w.c],
            crossed.at[k],
            sx_send.at[6 + k],
            sx_recv.at[6 + k],
            w.partner,
        )
        copy.start()
        pair_sum.append(copy)
    for n in range(2):
        for o in (1, -1):
            sum2[n, o].finish(grads.at[n, w.at2(axes[n][0], o, 0)])
        sum1[n].near()
    for k in range(4):
        pair_sum[k].wait_recv()
        add_rows(WIDTH, 32, ddense.at[2 * k + w.c], ddense.at[2 * k + w.c], crossed.at[k])
    xsum = RingSum(
        w, "x", lambda s: ddense.at[w.at("x", s)], WIDTH, x_relayed, x_landed, sx_send, sx_recv, 0
    )
    xsum.far()
    xsum.near()

    dn1 = contract_last(dqkv[:, 0:COLS], dense[0])
    for e in range(1, 6):
        dn1 = dn1 + contract_last(dqkv[:, e * COLS : (e + 1) * COLS], dense[e])
    x = x_ref[...].astype(F32)
    rho1 = lax.rsqrt(jnp.mean(x * x, axis=-1, keepdims=True) + NORM_EPS)
    r1 = x * rho1
    gain_grads[0:1] = jnp.sum(dn1 * r1, axis=0, keepdims=True)
    u1 = dn1 * gain[0:1]
    grad_tokens_ref[...] = h1[...] + rho1 * (
        u1 - r1 * jnp.mean(u1 * r1, axis=-1, keepdims=True)
    )
    for n in range(2):
        sum1[n].relay()
    xsum.relay()

    def bucket(b, n):
        hit = (buckets_ref[...] == b)[None]
        bias_rows[b] = jnp.sum(jnp.where(hit, ds_sum[...], 0.0), axis=1)
        return n

    lax.fori_loop(0, BUCKETS, bucket, 0)
    per_bucket = jnp.sum(bias_rows[...], axis=2)
    per_bucket = jnp.concatenate([per_bucket, jnp.zeros((BUCKETS, 4), F32)], axis=1)
    owner_f = owner_ref[...].astype(F32)
    grad_router = contract_first(n2[...], dlogits[...])
    wide = lax.dot_general(
        grad_router,
        fold_ref[...].astype(F32),
        (((1,), (1,)), ((), ())),
        precision=HIGH,
        preferred_element_type=F32,
    ) * group_ref[...].astype(F32)
    smalls = exact_dot(owner_f, wide)
    for n in range(2):
        smalls = smalls + lax.dot_general(
            owner_f * gain_grads[n : n + 1],
            gains_ref[n].astype(F32),
            (((1,), (1,)), ((), ())),
            precision=HIGH,
            preferred_element_type=F32,
        )
    table = table_ref[...].astype(F32)
    for j in range(4):
        smalls = smalls + exact_dot(
            table[:, j * 32 : (j + 1) * 32], exact_dot(per_bucket, pick_ref[j].astype(F32))
        )
    extra_mine[...] = smalls.reshape(DP, 8, 128)

    def extra_dp(k):
        peer = lax.rem(w.dp + k, DP)
        return remote(
            extra_mine.at[peer],
            dp_extra.at[w.dp],
            sdp_send.at[1, k],
            sdp_recv.at[1, k],
            {"dp": peer},
        )

    def start_extra(k, n):
        extra_dp(k).start()
        return n

    lax.fori_loop(1, DP, start_extra, 0)
    dp_extra[w.dp] = extra_mine[w.dp]
    for n in range(2):
        sum2[n, 0].finish(grads.at[n, w.dp])
    xsum.finish(ddense.at[w.e])

    def rows_of(dp):
        return pl.ds(pl.multiple_of(dp * ROWS, 16), ROWS)

    def dense_dp(k):
        peer = lax.rem(w.dp + k, DP)
        return remote(
            ddense.at[w.e, rows_of(peer)],
            dp_got.at[w.dp],
            sdp_send.at[0, k],
            sdp_recv.at[0, k],
            {"dp": peer},
        )

    def start_dense(k, n):
        dense_dp(k).start()
        return n

    def end_dense(k, n):
        for copy in (dense_dp(k), extra_dp(k)):
            copy.wait_recv()
            copy.wait_send()
        return n

    lax.fori_loop(1, DP, start_dense, 0)
    dp_got[w.dp] = ddense[w.e, rows_of(w.dp)]
    for n, ref in ((0, in_ref), (1, out_ref)):
        sum1[n].finish(ref)
    lax.fori_loop(1, DP, end_dense, 0)
    total = dp_got[0].astype(F32)
    extra_total = dp_extra[0]
    for k in range(1, DP):
        total = total + dp_got[k].astype(F32)
        extra_total = extra_total + dp_extra[k]
    extra_sum[...] = extra_total
    flat = jnp.concatenate([total[:, c * 128 : (c + 1) * 128] for c in range(3)], axis=0)
    last[...] = (
        jnp.dot(spread_ref[...], flat.astype(BF16), preferred_element_type=F32)
        .astype(BF16)
        .reshape(EXPERTS, 32, 128)
    )

    def to_owner(k):
        peer = lax.rem(w.e + k, EXPERTS)
        dev = {"expert": peer}
        return (
            remote(last.at[peer], last_got.at[w.e], sa_send.at[0, k], sa_recv.at[0, k], dev),
            remote(extra_sum, extra_got.at[w.e], sa_send.at[1, k], sa_recv.at[1, k], dev),
        )

    def start_owner(k, n):
        for copy in to_owner(k):
            copy.start()
        return n

    def end_owner(k, n):
        for copy in to_owner(k):
            copy.wait_recv()
            copy.wait_send()
        return n

    lax.fori_loop(1, EXPERTS, start_owner, 0)
    last_got[w.e] = last[w.e]
    extra_got[w.e] = extra_sum[...]
    lax.fori_loop(1, EXPERTS, end_owner, 0)
    dense_out_ref[...] = last_got[...].astype(F32)
    extra_total = extra_got[0]
    for k in range(1, EXPERTS):
        extra_total = extra_total + extra_got[k]
    extra_out_ref[...] = extra_total

    for copy in pair:
        copy.wait_send()
    ring.drain()
    for n in range(2):
        one[n].drain()
        for o in (0, -1, 1, 2):
            two[n, o].drain()
    for copy in pair_sum:
        copy.wait_send()
    xsum.drain()
    for n in range(2):
        sum1[n].drain()
        for o in order:
            sum2[n, o].drain()


def layer(x, cot, ids, slots, buckets, first, win, wout):
    hbm = pl.BlockSpec(memory_space=pl.ANY)
    vmem = pl.BlockSpec(memory_space=pltpu.VMEM)
    tokens = x.shape[0]
    half = SHARD // 2
    small = tuple(jnp.asarray(m, BF16) for m in (place_matrix(), spread_matrix(), *small_matrices()))

    def dma(*shape):
        return pltpu.SemaphoreType.DMA(shape)

    return pl.pallas_call(
        layer_kernel,
        out_shape=(
            jax.ShapeDtypeStruct((tokens, WIDTH), F32),
            jax.ShapeDtypeStruct((tokens, WIDTH), F32),
            jax.ShapeDtypeStruct((SHARD, WIDTH), F32),
            jax.ShapeDtypeStruct((SHARD, WIDTH), F32),
            jax.ShapeDtypeStruct((EXPERTS, 32, 128), F32),
            jax.ShapeDtypeStruct((8, 128), F32),
        ),
        in_specs=[vmem] * 14 + [hbm, hbm],
        out_specs=(vmem,) * 6,
        scratch_shapes=[
            pltpu.VMEM((2, DP, SHARD, WIDTH), BF16),
            pltpu.VMEM((EXPERTS, WIDTH, COLS), BF16),
            pltpu.VMEM((DP, 16, 128), BF16),
            pltpu.VMEM((EXPERTS, 48, 128), BF16),
            pltpu.VMEM((ROWS, COLS), BF16),
            pltpu.VMEM((16, 128), BF16),
            pltpu.VMEM((tokens, 3 * WIDTH), BF16),
            pltpu.VMEM((tokens, WIDTH), BF16),
            pltpu.VMEM((tokens, WIDTH), BF16),
            pltpu.VMEM((tokens, WIDTH), BF16),
            pltpu.VMEM((tokens, WIDTH), F32),
            pltpu.VMEM((tokens, 128), F32),
            pltpu.VMEM((tokens, 128), F32),
            pltpu.VMEM((2 * HEADS, LEN, LEN), F32),
            pltpu.VMEM((HEADS, LEN, LEN), F32),
            pltpu.VMEM((WIDTH, 128), BF16),
            pltpu.VMEM((8, WIDTH), F32),
            pltpu.VMEM((2, EXPERTS, 2, CAP, WIDTH), BF16),
            pltpu.VMEM((2, EXPERTS, 2, CAP, WIDTH), BF16),
            pltpu.VMEM((2, EXPERTS, 2, CAP, WIDTH), BF16),
            pltpu.VMEM((2, EXPERTS, 2, CAP, WIDTH), BF16),
            pltpu.VMEM((tokens, WIDTH), F32),
            pltpu.VMEM((tokens, WIDTH), F32),
            pltpu.VMEM((2, DP, SHARD, WIDTH), BF16),
            pltpu.VMEM((10, 2, half, WIDTH), BF16),
            pltpu.VMEM((10, 2, SHARD, WIDTH), BF16),
            pltpu.VMEM((EXPERTS, WIDTH, COLS), BF16),
            pltpu.VMEM((4, WIDTH, COLS), BF16),
            pltpu.VMEM((2, WIDTH // 2, COLS), BF16),
            pltpu.VMEM((2, WIDTH, COLS), BF16),
            pltpu.VMEM((DP, ROWS, COLS), BF16),
            pltpu.VMEM((DP, 8, 128), F32),
            pltpu.VMEM((DP, 8, 128), F32),
            pltpu.VMEM((8, 128), F32),
            pltpu.VMEM((EXPERTS, 32, 128), BF16),
            pltpu.VMEM((EXPERTS, 32, 128), BF16),
            pltpu.VMEM((EXPERTS, 8, 128), F32),
            pltpu.VMEM((tokens, WIDTH), BF16),
            pltpu.VMEM((tokens, WIDTH), BF16),
            pltpu.VMEM((tokens, 3 * WIDTH), BF16),
            pltpu.VMEM((HEADS, LEN, LEN), F32),
            pltpu.VMEM((tokens, 128), BF16),
            pltpu.VMEM((8, WIDTH), F32),
            pltpu.VMEM((BUCKETS, HEADS, LEN), F32),
            dma(2),
            dma(EXPERTS),
            dma(EXPERTS),
            dma(2, DP),
            dma(2, DP),
            dma(40),
            dma(40),
            dma(8),
            dma(8),
            dma(32),
            dma(32),
            dma(60),
            dma(60),
            dma(10),
            dma(10),
            dma(2, DP),
            dma(2, DP),
            dma(2, EXPERTS),
            dma(2, EXPERTS),
        ],
        compiler_params=pltpu.CompilerParams(
            collective_id=0, has_side_effects=True, vmem_limit_bytes=63 * MIB
        ),
        name="layer",
    )(x, cot, ids, slots, buckets, first, *small, win, wout)


def local(
    tokens,
    w_qkv,
    w_attn_out,
    w_router,
    gain_attn,
    gain_moe,
    bias_table,
    w_in,
    w_out,
    expert_ids,
    slots,
    buckets,
    cotangent,
):
    seqs = tokens.shape[0] // LEN
    me = lax.axis_index("expert")
    dense = jnp.concatenate([w_qkv, w_attn_out], axis=1)
    first = dense.reshape(6, EXPERTS, 3, 128).transpose(1, 2, 0, 3).reshape(EXPERTS, 18, 128)
    gap = jnp.zeros((2,), BF16)
    small = jnp.concatenate(
        [w_router.reshape(48), gain_attn, gap, gain_moe, gap, bias_table, jnp.zeros((61,), BF16)]
    )
    small = jnp.broadcast_to(small[None, None], (EXPERTS, 1, 128))
    first = jnp.concatenate(
        [first, jnp.zeros((EXPERTS, 14, 128), BF16), small, jnp.zeros((EXPERTS, 15, 128), BF16)],
        axis=1,
    )
    output, grad_tokens, grad_in, grad_out, dense_out, small = layer(
        tokens,
        cotangent,
        expert_ids.reshape(seqs, LEN),
        slots.reshape(seqs, LEN),
        buckets,
        first,
        w_in[0],
        w_out[0],
    )
    dense_out = dense_out[:, :18].reshape(EXPERTS, 3, 6, 128).transpose(2, 0, 1, 3)
    dense_out = dense_out.reshape(6, EXPERTS * COLS)
    small = lax.dynamic_index_in_dim(small, me, 0, keepdims=False)
    return (
        output,
        grad_tokens,
        dense_out[:, : 3 * WIDTH],
        dense_out[:, 3 * WIDTH :],
        small[:48].reshape(6, EXPERTS),
        small[48:54],
        small[56:62],
        small[64:67],
        grad_in[None],
        grad_out[None],
    )


def solution(mesh):
    spread = ("dp", "expert")
    in_specs = (
        P(spread, None),
        P(spread, None),
        P(spread, None),
        P(spread, None),
        P(spread),
        P(spread),
        P(spread),
        P("expert", "dp", None),
        P("expert", "dp", None),
        P(spread),
        P(spread),
        P(),
        P(spread, None),
    )
    out_specs = (
        P(spread, None),
        P(spread, None),
        P(spread, None),
        P(spread, None),
        P(spread, None),
        P(spread),
        P(spread),
        P(spread),
        P("expert", "dp", None),
        P("expert", "dp", None),
    )
    return jax.shard_map(local, mesh=mesh, in_specs=in_specs, out_specs=out_specs, check_vma=False)
```

time: 287 us -> 173 us (0.60)
  local copies, waits for them, and re-layouts: 61.6 us -> 11.5 us
  matrix products: 47 us -> 0 us
  other arithmetic: 13.3 us -> 1.53 us
  Pallas kernels: 162 us -> 159 us
    dot_general x24 -> x0, matrix products: 45.1 us -> none  [the longest x4 12.6 us: contract_first(): lax.dot_general(left, right, (((0,), (0,)), ((), ())), preferred_element_...]
    concatenate x7 -> x1, local copies, waits for them, and re-layouts: 11.7 us -> 0.1 us  [local(): jnp.concatenate([w_router.reshape(48), gain_attn, gap, gain_moe, gap, bia...]
    convert_element_type x5 -> x0, local copies, waits for them, and re-layouts: 9.8 us -> none  [the longest x1 6.65 us: local(): dgrads = jnp.concatenate([grad_qkv, grad_attn], axis=1).astype(BF16)]
    transpose x5 -> x0, local copies, waits for them, and re-layouts: 9.32 us -> none  [the longest x2 6.09 us: local(): wqkv = dense[:6].transpose(1, 0, 2).reshape(WIDTH, 3 * WIDTH)]
    unnamed x120 -> x20, local copies, waits for them, and re-layouts: 14.9 us -> 6.18 us
    slice x7 -> x2, local copies, waits for them, and re-layouts: 5.45 us -> 1.17 us  [the longest x1 0.59 us: local(): small[56:62]]
    pallas_call x4 -> x1, Pallas kernels: 162 us -> 159 us  [layer(): pl.pallas_call(layer_kernel, out_shape=(jax.ShapeDtypeStruct((tokens, WID...]
    concatenate x2 -> x0, other arithmetic: 3.55 us -> none  [the longest x1 2.79 us: local(): dgrads = jnp.concatenate([grad_qkv, grad_attn], axis=1).astype(BF16)]
where the time goes in v2:
time: 173 us; the launch traced here: 172 us
  Pallas kernels  159 us (92%)
  local copies, waits for them, and re-layouts  11.5 us (7%)
    pallas_call x1, Pallas kernels, layer(): pl.pallas_call(layer_kernel, out_shape=(jax.ShapeDtypeStruct((tokens, WID...  159 us
    unnamed x20, local copies, waits for them, and re-layouts  6.18 us

profile of v2, /device:TPU:1, one launch (start us, length us, event | category | flops | bytes accessed | tf_op | source)
XLA Modules:
  0.0 172.4 jit_solution(2358958144166412607)
XLA Ops:
  0.6 0.8 pad_maximum_fusion
  1.4 0.1 reshape.54
  1.6 0.7 copy-done.4
  2.2 0.1 reshape.56
  2.3 0.6 copy-done.5
  3.0 0.1 concatenate.10
  3.1 0.1 pad.1.clone
  3.2 0.1 pad.3.clone
  3.3 0.7 maximum_maximum_fusion.first_ref
  4.0 158.7 %layer.1 = (f32[256,768]{1,0:T(8,128)}, f32[256,768]{1,0:T(8,128)}, f32[192,768]{1,0:T(8,128)}, f32[192,768]{1,0:T(8,128)}, f32[8,32,128]{2,1,0:T(8,128)}, /*index=5*/f32[8,128]{1,0:T(8,128)}) custom-call(bf16[256,768]{1,0:T(8,128)(2,1)} %x_ref.1, f32[256,768]{1,0:T(8,128)} %cot_ref.1, s32[2,128]{1,0:T(2,128)} %bitcast.24, s32[2,128]{1,0:T(2,128)} %bitcast.25, ...), custom_call_target="tpu_custom_call" | custom-call | tf_op jit(solution)/shard_map/layer/pallas_call | solution.py:908
  162.7 0.8 constant_dynamic-slice_fusion
  163.4 0.6 slice_bitcast_fusion.1
  164.0 0.7 reshape.59
  164.7 0.6 slice_bitcast_fusion
  165.3 0.9 slice.31
  166.3 0.6 slice.41
  166.9 0.6 slice.42
  167.6 0.9 copy.43
  168.4 0.5 copy-done
  169.0 0.9 copy.44
  169.9 0.5 copy-done.3
  170.3 0.8 copy.45
  171.1 0.5 copy-done.2
  171.6 0.8 copy.46
  (22 shorter events, 0.2 us)
Async XLA Ops:
  1.5 0.7 copy-start.4
  2.3 0.7 copy-start.5
  2.3 0.7 copy-start.6
  2.3 0.7 copy-start.7
  162.7 4.9 %copy-start.1 = (f32[256,768]{1,0:T(8,128)S(1)}, f32[256,768]{1,0:T(8,128)}, u32[]{:S(2)}) copy-start(f32[256,768]{1,0:T(8,128)} %get-tuple-element.34) | copy-start | bytes 2359300
  167.6 1.4 copy-start
  169.0 1.3 copy-start.3
  170.3 1.3 copy-start.2

commit v3 on v2

--- a/solution.py
+++ b/solution.py
@@ -94,7 +94,7 @@
         return lax.rem(self.z + dz + 4, 4) * 4 + lax.rem(self.y + dy + 4, 4)
 
 
-def greet(w, dp_too):
+def greet(w):
     barrier = pltpu.get_barrier_semaphore()
 
     def hello_e(k, n):
@@ -110,15 +110,54 @@
         return n
 
     lax.fori_loop(1, EXPERTS, hello_e, 0)
-    if dp_too:
-        lax.fori_loop(1, DP, hello_dp, 0)
-    pl.semaphore_wait(barrier, EXPERTS - 1 + (DP - 1 if dp_too else 0))
+    lax.fori_loop(1, DP, hello_dp, 0)
 
 
 def remote(src, dst, send, recv, dev):
     return pltpu.make_async_remote_copy(
         src_ref=src, dst_ref=dst, send_sem=send, recv_sem=recv, device_id=dev, device_id_type=MESH
     )
+
+
+class FineRingGather:
+    def __init__(self, w, axis, place, rows, send, recv):
+        self.w, self.axis, self.place, self.half = w, axis, place, rows // 2
+        self.send, self.recv = send, recv
+        self.copies = []
+
+    def _go(self, step, place, k):
+        part = place.at[pl.ds(k * self.half, self.half)]
+        n = len(self.copies)
+        copy = remote(
+            part, part, self.send.at[n], self.recv.at[n], self.w.dev(self.axis, step)
+        )
+        copy.start()
+        self.copies.append(copy)
+
+    def start(self):
+        own = self.place(0)
+        self._go(1, own, 0)
+        self._go(-1, own, 1)
+        self._go(1, own, 1)
+        self._go(-1, own, 0)
+
+    def relay(self):
+        self.copies[0].wait_recv()
+        self._go(1, self.place(-1), 0)
+        self.copies[1].wait_recv()
+        self._go(-1, self.place(1), 1)
+
+    def near(self):
+        self.copies[2].wait_recv()
+        self.copies[3].wait_recv()
+
+    def finish(self):
+        self.copies[4].wait_recv()
+        self.copies[5].wait_recv()
+
+    def drain(self):
+        for copy in self.copies:
+            copy.wait_send()
 
 
 class RingGather:
@@ -178,6 +217,7 @@
         self.w, self.axis, self.place, self.rows, self.half = w, axis, place, rows, rows // 2
         self.relayed, self.landed = relayed, landed
         self.send, self.recv, self.base = send, recv, base
+        self.step = min(32, self.half)
         self.copies = {}
 
     def _go(self, k, src, dst, step):
@@ -205,17 +245,17 @@
     def relay(self):
         self.copies[0].wait_recv()
         low = self._part(self.place(1), 0)
-        add_rows(self.half, 32, low, low, self.relayed.at[0])
+        add_rows(self.half, self.step, low, low, self.relayed.at[0])
         self._go(4, low, self._part(self.landed.at[0], 0), 1)
         self.copies[1].wait_recv()
         high = self._part(self.place(-1), 1)
-        add_rows(self.half, 32, high, high, self.relayed.at[1])
+        add_rows(self.half, self.step, high, high, self.relayed.at[1])
         self._go(5, high, self._part(self.landed.at[1], 1), -1)
 
     def finish(self, dst):
         for k in (2, 3, 4, 5):
             self.copies[k].wait_recv()
-        add_rows(self.rows, 32, dst, self.place(0), self.landed.at[0], self.landed.at[1])
+        add_rows(self.rows, self.step, dst, self.place(0), self.landed.at[0], self.landed.at[1])
 
     def drain(self):
         for k in range(6):
@@ -244,11 +284,39 @@
 
 
 def layer_kernel(
+    x_hbm,
+    cot_hbm,
+    ids_hbm,
+    slots_hbm,
+    buckets_hbm,
+    wqkv_ref,
+    wattn_ref,
+    wrouter_ref,
+    small_ref,
+    place_hbm,
+    spread_hbm,
+    owner_hbm,
+    gains_hbm,
+    group_hbm,
+    fold_hbm,
+    table_hbm,
+    pick_hbm,
+    win_ref,
+    wout_ref,
+    output_hbm,
+    grad_tokens_hbm,
+    in_hbm,
+    out_hbm,
+    grad_qkv_ref,
+    grad_attn_ref,
+    router_out_ref,
+    extra_out_ref,
     x_ref,
     cot_ref,
     ids_ref,
     slots_ref,
     buckets_ref,
+    first_f,
     first_ref,
     place_ref,
     spread_ref,
@@ -258,14 +326,10 @@
     fold_ref,
     table_ref,
     pick_ref,
-    win_ref,
-    wout_ref,
     output_ref,
     grad_tokens_ref,
     in_ref,
     out_ref,
-    dense_out_ref,
-    extra_out_ref,
     weights,
     dense,
     extra,
@@ -293,10 +357,18 @@
     relayed,
     landed,
     ddense,
+    dthird,
     crossed,
+    crossed_third,
     x_relayed,
     x_landed,
     dp_got,
+    third_relayed,
+    third_landed,
+    third_relayed_y,
+    third_landed_y,
+    third_sum,
+    third_last,
     dp_extra,
     extra_mine,
     extra_sum,
@@ -310,6 +382,8 @@
     dlogits,
     gain_grads,
     bias_rows,
+    load_sem,
+    store_sem,
     own_sem,
     a2a_send,
     a2a_recv,
@@ -329,10 +403,56 @@
     sdp_recv,
     sa_send,
     sa_recv,
+    st_send,
+    st_recv,
 ):
     w = Where()
     scale = HEAD_DIM ** (-0.5)
-    greet(w, True)
+    loads = [
+        pltpu.make_async_copy(src, dst, load_sem.at[k])
+        for k, (src, dst) in enumerate(
+            (
+                (fold_hbm, fold_ref),
+                (place_hbm, place_ref),
+                (x_hbm, x_ref),
+                (owner_hbm, owner_ref),
+                (gains_hbm, gains_ref),
+                (group_hbm, group_ref),
+                (table_hbm, table_ref),
+                (buckets_hbm, buckets_ref),
+                (ids_hbm, ids_ref),
+                (slots_hbm, slots_ref),
+                (cot_hbm, cot_ref),
+                (pick_hbm, pick_ref),
+                (spread_hbm, spread_ref),
+            )
+        )
+    ]
+    for load in loads:
+        load.start()
+    stores = []
+
+    def store(src, dst):
+        copy = pltpu.make_async_copy(src, dst, store_sem.at[len(stores)])
+        copy.start()
+        stores.append(copy)
+
+    greet(w)
+    loads[0].wait()
+
+    first_f[...] = jnp.zeros_like(first_f)
+    lane = lax.broadcasted_iota(jnp.int32, (6, 128), 1)
+    turn = 8 * lax.broadcasted_iota(jnp.int32, (6, 128), 0)
+    routed = contract_last(wrouter_ref[...], fold_ref[:, :EXPERTS])
+    routed = jnp.where((lane >= turn) & (lane < turn + 8), routed, 0.0)
+    row = jnp.sum(routed, axis=0, keepdims=True) + small_ref[...].astype(F32)
+    for e in range(EXPERTS):
+        ref, at = (wqkv_ref, e * COLS) if e < 6 else (wattn_ref, (e - 6) * COLS)
+        for c in range(3):
+            first_f[e, c * 6 : c * 6 + 6] = ref[:, at + c * 128 : at + (c + 1) * 128].astype(F32)
+        first_f[e, 32:33] = row
+    first_ref[...] = first_f[...].astype(BF16)
+    pl.semaphore_wait(pltpu.get_barrier_semaphore(), EXPERTS - 1 + DP - 1)
 
     def to_expert(k):
         peer = lax.rem(w.e + k, EXPERTS)
@@ -375,6 +495,8 @@
             )
     for n in range(2):
         one[n].start()
+    for load in loads[1:]:
+        load.wait()
 
     def end_a2a(k, n):
         copy = to_expert(k)
@@ -417,11 +539,11 @@
     x = x_ref[...].astype(F32)
     rho1 = lax.rsqrt(jnp.mean(x * x, axis=-1, keepdims=True) + NORM_EPS)
     lax.fori_loop(1, DP, end_dp, 0)
-    ring = RingGather(w, "x", lambda s: dense.at[w.at("x", s)], WIDTH, x_send, x_recv, 0)
+    ring = FineRingGather(w, "x", lambda s: dense.at[w.at("x", s)], WIDTH, x_send, x_recv)
     ring.start()
 
     def across(k, ref):
-        copy = remote(ref, ref, x_send.at[4 + k], x_recv.at[4 + k], w.partner)
+        copy = remote(ref, ref, x_send.at[6 + k], x_recv.at[6 + k], w.partner)
         copy.start()
         return copy
 
@@ -450,6 +572,7 @@
     n1[...] = (x * rho1 * gain[0:1]).astype(BF16)
 
     ring.relay()
+    ring.near()
     pair.append(across(1, dense.at[w.at("x", -1)]))
     pair.append(across(2, dense.at[w.at("x", 1)]))
     for n in range(2):
@@ -577,33 +700,6 @@
         wait_tokens(sent, arrived, 0, s)
     for copy in owns:
         copy.wait()
-
-    slots_here = 2 * EXPERTS * CAP
-    eo[...] = jnp.zeros_like(eo)
-    dn2e[...] = jnp.zeros_like(dn2e)
-
-    def hidden_block(j, n):
-        block = pl.ds(2 * j, 2)
-        w_in = weights[0, block].reshape(2 * SHARD, WIDTH)
-        w_out = weights[1, block].reshape(2 * SHARD, WIDTH)
-        rows = arrived[:, :, 0].reshape(slots_here, WIDTH)
-        drows = arrived[:, :, 1].reshape(slots_here, WIDTH)
-        act, slope = gelu_both(contract_last(rows, w_in))
-        hid = act.astype(BF16)
-        dpre = (contract_last(drows, w_out) * slope).astype(BF16)
-        eo[...] += jnp.dot(hid, w_out, preferred_element_type=F32)
-        dn2e[...] += jnp.dot(dpre, w_in, preferred_element_type=F32)
-        grads[0, block] = contract_first(dpre, rows).astype(BF16).reshape(2, SHARD, WIDTH)
-        grads[1, block] = contract_first(hid, drows).astype(BF16).reshape(2, SHARD, WIDTH)
-        return n
-
-    lax.fori_loop(0, DP // 2, hidden_block, 0)
-    for s in range(2):
-        for e in range(EXPERTS):
-            rows = pl.ds((s * EXPERTS + e) * CAP, CAP)
-            back[s, e, 0] = eo[rows].astype(BF16)
-            back[s, e, 1] = dn2e[rows].astype(BF16)
-        send_tokens(back, returned, 16, s)
 
     axes = (("y", "z"), ("z", "y"))
     order = (2, 1, -1, 0)
@@ -632,9 +728,46 @@
             sum_recv,
             (n * 5 + 4) * 6,
         )
+    slots_here = 2 * EXPERTS * CAP
+    eo[...] = jnp.zeros_like(eo)
+    dn2e[...] = jnp.zeros_like(dn2e)
+
+
+    def hidden_blocks(one_of, other_of):
+        def body(i, n):
+            at = [w.at2("y", dy, dz) for dz, dy in (one_of(i), other_of(i))]
+            w_in = jnp.concatenate([weights[0, k] for k in at], axis=0)
+            w_out = jnp.concatenate([weights[1, k] for k in at], axis=0)
+            rows = arrived[:, :, 0].reshape(slots_here, WIDTH)
+            drows = arrived[:, :, 1].reshape(slots_here, WIDTH)
+            act, slope = gelu_both(contract_last(rows, w_in))
+            hid = act.astype(BF16)
+            dpre = (contract_last(drows, w_out) * slope).astype(BF16)
+            eo[...] += jnp.dot(hid, w_out, preferred_element_type=F32)
+            dn2e[...] += jnp.dot(dpre, w_in, preferred_element_type=F32)
+            for m, value in enumerate((contract_first(dpre, rows), contract_first(hid, drows))):
+                value = value.astype(BF16)
+                for k in range(2):
+                    grads[m, at[k]] = value[k * SHARD : (k + 1) * SHARD]
+            return n
+
+        lax.fori_loop(0, 2, body, 0)
+
+    hidden_blocks(lambda i: (2, 2 * i), lambda i: (2, 2 * i + 1))
     for o in order:
-        for n in range(2):
-            sum2[n, o].far()
+        sum2[0, o].far()
+    hidden_blocks(lambda i: (3 * i, 2), lambda i: (1, 2 - 2 * i))
+    for o in order:
+        sum2[1, o].far()
+    hidden_blocks(lambda i: (0, i), lambda i: (3, i))
+    hidden_blocks(lambda i: (1, 1 + 2 * i), lambda i: (3 * i, 3))
+    for s in (1, 0):
+        for e in range(EXPERTS):
+            rows = pl.ds((s * EXPERTS + e) * CAP, CAP)
+            back[s, e, 0] = eo[rows].astype(BF16)
+            back[s, e, 1] = dn2e[rows].astype(BF16)
+        send_tokens(back, returned, 16, s)
+
     for o in order:
         for n in range(2):
             sum2[n, o].near()
@@ -649,6 +782,7 @@
         combined = contract_first(route, returned[s, :, 0].reshape(LEN, WIDTH))
         g, cot, h = gate[rows, 0:1], cot_ref[rows], h1[rows]
         output_ref[rows] = h + g * combined
+        store(output_ref.at[rows], output_hbm.at[rows])
         dgate = jnp.sum(cot * combined, axis=-1, keepdims=True)
         dl = (probs[rows] * (hot - g) * dgate).astype(BF16)
         dlogits[rows] = dl
@@ -700,46 +834,83 @@
 
     wait_tokens(back, returned, 16, 1)
     second_norm_back(1)
-    attention_back(1, 0, 3)
-    for o in (1, -1):
+    for o in (1, -1, 0):
         for n in range(2):
             sum2[n, o].relay()
+    attention_back(1, 0, 3)
     wait_tokens(back, returned, 16, 0)
     second_norm_back(0)
+    attention_back(0, 0, 3)
+
+    third = 2 * COLS // 3
+
+    def dense_block(e, value):
+        value = value.astype(BF16)
+        ddense[e] = value[:, :third]
+        dthird[e % 2, :, e // 2] = value[:, third:].reshape(DP, ROWS, COLS - third)
+
+    for e in range(6):
+        dense_block(e, contract_first(n1[...], dqkv[:, e * COLS : (e + 1) * COLS]))
     for e in range(2):
-        ddense[6 + e] = contract_first(attn[...], da[:, e * COLS : (e + 1) * COLS]).astype(BF16)
-    for n in range(2):
-        sum2[n, 0].relay()
-    attention_back(0, 0, 3)
-    for n in range(2):
-        sum2[n, 2].finish(grads.at[n, w.at2(axes[n][0], 2, 0)])
-        sum1[n].far()
-    for e in range(6):
-        ddense[e] = contract_first(n1[...], dqkv[:, e * COLS : (e + 1) * COLS]).astype(BF16)
-
+        dense_block(6 + e, contract_first(attn[...], da[:, e * COLS : (e + 1) * COLS]))
+
+    pair_third = remote(
+        dthird.at[1 - w.c], crossed_third, sx_send.at[10], sx_recv.at[10], w.partner
+    )
+    pair_third.start()
     pair_sum = []
-    for k in range(4):
+    for k, o in enumerate(order):
+        to = lax.rem(w.x + o + 4, 4)
         copy = remote(
-            ddense.at[2 * k + 1 - w.c],
-            crossed.at[k],
+            ddense.at[2 * to + 1 - w.c],
+            crossed.at[to],
             sx_send.at[6 + k],
             sx_recv.at[6 + k],
             w.partner,
         )
         copy.start()
         pair_sum.append(copy)
-    for n in range(2):
-        for o in (1, -1):
-            sum2[n, o].finish(grads.at[n, w.at2(axes[n][0], o, 0)])
-        sum1[n].near()
-    for k in range(4):
+
+    def third_rows(s):
+        return dthird.at[w.c, pl.ds(4 * lax.rem(w.z + s + 4, 4), 4)]
+
+    zsum = RingSum(w, "z", third_rows, 4, third_relayed, third_landed, st_send, st_recv, 3)
+    ysum = RingSum(
+        w,
+        "y",
+        lambda s: dthird.at[w.c, w.at("y", s)],
+        4,
+        third_relayed_y,
+        third_landed_y,
+        st_send,
+        st_recv,
+        9,
+    )
+
+    def add_third(k, n):
+        total = dthird[w.c, k].astype(F32) + crossed_third[k].astype(F32)
+        dthird[w.c, k] = total.astype(BF16)
+        return n
+
+    def add_pair(k):
         pair_sum[k].wait_recv()
-        add_rows(WIDTH, 32, ddense.at[2 * k + w.c], ddense.at[2 * k + w.c], crossed.at[k])
+        to = lax.rem(w.x + order[k] + 4, 4)
+        here = ddense.at[2 * to + w.c]
+        add_rows(WIDTH, 32, here, here, crossed.at[to])
+
+    pair_third.wait_recv()
+    lax.fori_loop(0, DP, add_third, 0)
+    zsum.far()
+    zsum.near()
     xsum = RingSum(
         w, "x", lambda s: ddense.at[w.at("x", s)], WIDTH, x_relayed, x_landed, sx_send, sx_recv, 0
     )
+    add_pair(0)
     xsum.far()
+    add_pair(1)
+    add_pair(2)
     xsum.near()
+    add_pair(3)
 
     dn1 = contract_last(dqkv[:, 0:COLS], dense[0])
     for e in range(1, 6):
@@ -752,9 +923,11 @@
     grad_tokens_ref[...] = h1[...] + rho1 * (
         u1 - r1 * jnp.mean(u1 * r1, axis=-1, keepdims=True)
     )
-    for n in range(2):
-        sum1[n].relay()
-    xsum.relay()
+    store(grad_tokens_ref, grad_tokens_hbm)
+    zsum.relay()
+    for n in range(2):
+        sum2[n, 2].finish(grads.at[n, w.at2(axes[n][0], 2, 0)])
+        sum1[n].far()
 
     def bucket(b, n):
         hit = (buckets_ref[...] == b)[None]
@@ -805,8 +978,32 @@
 
     lax.fori_loop(1, DP, start_extra, 0)
     dp_extra[w.dp] = extra_mine[w.dp]
+    zsum.finish(third_rows(0))
+    ysum.far()
+    ysum.near()
+    xsum.relay()
+    for n in range(2):
+        for o in (1, -1):
+            sum2[n, o].finish(grads.at[n, w.at2(axes[n][0], o, 0)])
+        sum1[n].near()
+    for n in range(2):
+        sum1[n].relay()
     for n in range(2):
         sum2[n, 0].finish(grads.at[n, w.dp])
+    ysum.relay()
+    ysum.finish(third_sum)
+    third_x = []
+    for k, o in enumerate((2, 1, -1)):
+        copy = remote(
+            third_sum.at[lax.rem(w.x + o + 4, 4)],
+            third_last.at[w.x],
+            st_send.at[k],
+            st_recv.at[k],
+            w.dev("x", o),
+        )
+        copy.start()
+        third_x.append(copy)
+    third_last[w.x] = third_sum[w.x]
     xsum.finish(ddense.at[w.e])
 
     def rows_of(dp):
@@ -834,8 +1031,14 @@
 
     lax.fori_loop(1, DP, start_dense, 0)
     dp_got[w.dp] = ddense[w.e, rows_of(w.dp)]
-    for n, ref in ((0, in_ref), (1, out_ref)):
+    for n, (ref, hbm) in enumerate(((in_ref, in_hbm), (out_ref, out_hbm))):
         sum1[n].finish(ref)
+        store(ref, hbm)
+    for copy in third_x:
+        copy.wait_recv()
+    last_third = third_last[0].astype(F32)
+    for k in range(1, 4):
+        last_third = last_third + third_last[k].astype(F32)
     lax.fori_loop(1, DP, end_dense, 0)
     total = dp_got[0].astype(F32)
     extra_total = dp_extra[0]
@@ -843,7 +1046,7 @@
         total = total + dp_got[k].astype(F32)
         extra_total = extra_total + dp_extra[k]
     extra_sum[...] = extra_total
-    flat = jnp.concatenate([total[:, c * 128 : (c + 1) * 128] for c in range(3)], axis=0)
+    flat = jnp.concatenate([total[:, :128], total[:, 128:], last_third], axis=0)
     last[...] = (
         jnp.dot(spread_ref[...], flat.astype(BF16), preferred_element_type=F32)
         .astype(BF16)
@@ -873,11 +1076,20 @@
     last_got[w.e] = last[w.e]
     extra_got[w.e] = extra_sum[...]
     lax.fori_loop(1, EXPERTS, end_owner, 0)
-    dense_out_ref[...] = last_got[...].astype(F32)
+    for e in range(EXPERTS):
+        columns = last_got[e].astype(F32)
+        for c in range(3):
+            ref = grad_qkv_ref if e < 6 else grad_attn_ref
+            at = (e % 6 if e < 6 else e - 6) * COLS + c * 128
+            ref[:, at : at + 128] = columns[c * 6 : c * 6 + 6]
     extra_total = extra_got[0]
     for k in range(1, EXPERTS):
         extra_total = extra_total + extra_got[k]
-    extra_out_ref[...] = extra_total
+    extra_sum[...] = extra_total
+    row = extra_sum[pl.ds(w.e, 1)]
+    extra_out_ref[...] = row
+    for r in range(6):
+        router_out_ref[r : r + 1] = row[:, r * EXPERTS : (r + 1) * EXPERTS]
 
     for copy in pair:
         copy.wait_send()
@@ -886,20 +1098,24 @@
         one[n].drain()
         for o in (0, -1, 1, 2):
             two[n, o].drain()
-    for copy in pair_sum:
+    for copy in (*pair_sum, pair_third, *third_x):
         copy.wait_send()
     xsum.drain()
+    zsum.drain()
+    ysum.drain()
+    for copy in stores:
+        copy.wait()
     for n in range(2):
         sum1[n].drain()
         for o in order:
             sum2[n, o].drain()
 
 
-def layer(x, cot, ids, slots, buckets, first, win, wout):
+def layer(x, cot, ids, slots, buckets, wqkv, wattn, wrouter, row, win, wout):
     hbm = pl.BlockSpec(memory_space=pl.ANY)
     vmem = pl.BlockSpec(memory_space=pltpu.VMEM)
     tokens = x.shape[0]
-    half = SHARD // 2
+    half, main = SHARD // 2, COLS - 128
     small = tuple(jnp.asarray(m, BF16) for m in (place_matrix(), spread_matrix(), *small_matrices()))
 
     def dma(*shape):
@@ -912,12 +1128,22 @@
             jax.ShapeDtypeStruct((tokens, WIDTH), F32),
             jax.ShapeDtypeStruct((SHARD, WIDTH), F32),
             jax.ShapeDtypeStruct((SHARD, WIDTH), F32),
-            jax.ShapeDtypeStruct((EXPERTS, 32, 128), F32),
-            jax.ShapeDtypeStruct((8, 128), F32),
+            jax.ShapeDtypeStruct((6, 3 * WIDTH), F32),
+            jax.ShapeDtypeStruct((6, WIDTH), F32),
+            jax.ShapeDtypeStruct((6, EXPERTS), F32),
+            jax.ShapeDtypeStruct((1, 128), F32),
         ),
-        in_specs=[vmem] * 14 + [hbm, hbm],
-        out_specs=(vmem,) * 6,
+        in_specs=[hbm] * 5 + [vmem] * 4 + [hbm] * 10,
+        out_specs=(hbm,) * 4 + (vmem,) * 4,
         scratch_shapes=[
+            *(pltpu.VMEM(a.shape, a.dtype) for a in (x, cot, ids, slots, buckets)),
+            pltpu.VMEM((EXPERTS, ROWS, 128), F32),
+            pltpu.VMEM((EXPERTS, ROWS, 128), BF16),
+            *(pltpu.VMEM(a.shape, a.dtype) for a in small),
+            pltpu.VMEM((tokens, WIDTH), F32),
+            pltpu.VMEM((tokens, WIDTH), F32),
+            pltpu.VMEM((SHARD, WIDTH), F32),
+            pltpu.VMEM((SHARD, WIDTH), F32),
             pltpu.VMEM((2, DP, SHARD, WIDTH), BF16),
             pltpu.VMEM((EXPERTS, WIDTH, COLS), BF16),
             pltpu.VMEM((DP, 16, 128), BF16),
@@ -944,11 +1170,19 @@
             pltpu.VMEM((2, DP, SHARD, WIDTH), BF16),
             pltpu.VMEM((10, 2, half, WIDTH), BF16),
             pltpu.VMEM((10, 2, SHARD, WIDTH), BF16),
-            pltpu.VMEM((EXPERTS, WIDTH, COLS), BF16),
-            pltpu.VMEM((4, WIDTH, COLS), BF16),
-            pltpu.VMEM((2, WIDTH // 2, COLS), BF16),
-            pltpu.VMEM((2, WIDTH, COLS), BF16),
-            pltpu.VMEM((DP, ROWS, COLS), BF16),
+            pltpu.VMEM((EXPERTS, WIDTH, main), BF16),
+            pltpu.VMEM((2, DP, 4, ROWS, 128), BF16),
+            pltpu.VMEM((4, WIDTH, main), BF16),
+            pltpu.VMEM((DP, 4, ROWS, 128), BF16),
+            pltpu.VMEM((2, WIDTH // 2, main), BF16),
+            pltpu.VMEM((2, WIDTH, main), BF16),
+            pltpu.VMEM((DP, ROWS, main), BF16),
+            pltpu.VMEM((2, 2, 4, ROWS, 128), BF16),
+            pltpu.VMEM((2, 4, 4, ROWS, 128), BF16),
+            pltpu.VMEM((2, 2, ROWS, 128), BF16),
+            pltpu.VMEM((2, 4, ROWS, 128), BF16),
+            pltpu.VMEM((4, ROWS, 128), BF16),
+            pltpu.VMEM((4, ROWS, 128), BF16),
             pltpu.VMEM((DP, 8, 128), F32),
             pltpu.VMEM((DP, 8, 128), F32),
             pltpu.VMEM((8, 128), F32),
@@ -962,6 +1196,8 @@
             pltpu.VMEM((tokens, 128), BF16),
             pltpu.VMEM((8, WIDTH), F32),
             pltpu.VMEM((BUCKETS, HEADS, LEN), F32),
+            dma(13),
+            dma(5),
             dma(2),
             dma(EXPERTS),
             dma(EXPERTS),
@@ -969,24 +1205,55 @@
             dma(2, DP),
             dma(40),
             dma(40),
-            dma(8),
-            dma(8),
+            dma(10),
+            dma(10),
             dma(32),
             dma(32),
             dma(60),
             dma(60),
-            dma(10),
-            dma(10),
+            dma(11),
+            dma(11),
             dma(2, DP),
             dma(2, DP),
             dma(2, EXPERTS),
             dma(2, EXPERTS),
+            dma(15),
+            dma(15),
         ],
         compiler_params=pltpu.CompilerParams(
             collective_id=0, has_side_effects=True, vmem_limit_bytes=63 * MIB
         ),
         name="layer",
-    )(x, cot, ids, slots, buckets, first, *small, win, wout)
+    )(x, cot, ids, slots, buckets, wqkv, wattn, wrouter, row, *small, win, wout)
+
+
+def hand_over_kernel(*refs):
+    n = len(refs) // 3
+    sems = refs[-1]
+    come = [pltpu.make_async_copy(refs[k], refs[2 * n + k], sems.at[0, k]) for k in range(n)]
+    go = [pltpu.make_async_copy(refs[2 * n + k], refs[n + k], sems.at[1, k]) for k in range(n)]
+    for copy in come:
+        copy.start()
+    for k in range(n):
+        come[k].wait()
+        go[k].start()
+    for copy in go:
+        copy.wait()
+
+
+def hand_over(*arrays):
+    hbm = pl.BlockSpec(memory_space=pl.ANY)
+    return pl.pallas_call(
+        hand_over_kernel,
+        out_shape=tuple(jax.ShapeDtypeStruct(a.shape, a.dtype) for a in arrays),
+        in_specs=[hbm] * len(arrays),
+        out_specs=(hbm,) * len(arrays),
+        scratch_shapes=[
+            *(pltpu.VMEM(a.shape, a.dtype) for a in arrays),
+            pltpu.SemaphoreType.DMA((2, len(arrays))),
+        ],
+        name="hand_over",
+    )(*arrays)
 
 
 def local(
@@ -1005,37 +1272,33 @@
     cotangent,
 ):
     seqs = tokens.shape[0] // LEN
-    me = lax.axis_index("expert")
-    dense = jnp.concatenate([w_qkv, w_attn_out], axis=1)
-    first = dense.reshape(6, EXPERTS, 3, 128).transpose(1, 2, 0, 3).reshape(EXPERTS, 18, 128)
     gap = jnp.zeros((2,), BF16)
-    small = jnp.concatenate(
-        [w_router.reshape(48), gain_attn, gap, gain_moe, gap, bias_table, jnp.zeros((61,), BF16)]
+    row = jnp.concatenate(
+        [jnp.zeros((48,), BF16), gain_attn, gap, gain_moe, gap, bias_table, jnp.zeros((61,), BF16)]
     )
-    small = jnp.broadcast_to(small[None, None], (EXPERTS, 1, 128))
-    first = jnp.concatenate(
-        [first, jnp.zeros((EXPERTS, 14, 128), BF16), small, jnp.zeros((EXPERTS, 15, 128), BF16)],
-        axis=1,
-    )
-    output, grad_tokens, grad_in, grad_out, dense_out, small = layer(
+    results = layer(
         tokens,
         cotangent,
         expert_ids.reshape(seqs, LEN),
         slots.reshape(seqs, LEN),
         buckets,
-        first,
+        w_qkv,
+        w_attn_out,
+        w_router,
+        row[None],
         w_in[0],
         w_out[0],
     )
-    dense_out = dense_out[:, :18].reshape(EXPERTS, 3, 6, 128).transpose(2, 0, 1, 3)
-    dense_out = dense_out.reshape(6, EXPERTS * COLS)
-    small = lax.dynamic_index_in_dim(small, me, 0, keepdims=False)
+    output, grad_tokens, grad_in, grad_out, grad_qkv, grad_attn, grad_router = hand_over(
+        *results[:7]
+    )
+    small = results[7][0]
     return (
         output,
         grad_tokens,
-        dense_out[:, : 3 * WIDTH],
-        dense_out[:, 3 * WIDTH :],
-        small[:48].reshape(6, EXPERTS),
+        grad_qkv,
+        grad_attn,
+        grad_router,
         small[48:54],
         small[56:62],
         small[64:67],

time: 173 us -> 153 us (0.88)
  Pallas kernels: 159 us -> 149 us
  local copies, waits for them, and re-layouts: 11.5 us -> 3.04 us
    pallas_call x1, Pallas kernels: 159 us -> 146 us  [layer(): pl.pallas_call(layer_kernel, out_shape=(jax.ShapeDtypeStruct((tokens, WID...]
    unnamed x20 -> x8, local copies, waits for them, and re-layouts: 6.18 us -> 1.26 us
    pallas_call x0 -> x1, Pallas kernels: none -> 2.8 us  [hand_over(): pl.pallas_call(hand_over_kernel, out_shape=tuple((jax.ShapeDtypeStruct(a....]
    slice x5 -> x0, local copies, waits for them, and re-layouts: 2.18 us -> none  [the longest x2 0.92 us: local(): dense_out[:, :18].reshape(EXPERTS, 3, 6, 128).transpose(2, 0, 1, 3)]
where the time goes in v3:
time: 153 us
  Pallas kernels  149 us (97%)
  local copies, waits for them, and re-layouts  3.04 us (2%)
    pallas_call x1, Pallas kernels, layer(): pl.pallas_call(layer_kernel, out_shape=(jax.ShapeDtypeStruct((tokens, WID...  146 us

profile of v3, /device:TPU:1, one launch (start us, length us, event | category | flops | bytes accessed | tf_op | source)
XLA Modules:
  0.0 152.8 jit_solution(4864338513950177790)
XLA Ops:
  0.7 0.0 copy-start.1
  0.7 0.0 copy-start.2
  0.7 0.0 copy-start.3
  0.7 0.6 copy-done.1
  1.3 0.0 copy-done.2
  1.3 0.0 copy-done.3
  1.4 0.6 concatenate.3
  2.0 146.3 %layer.1 = (f32[256,768]{1,0:T(8,128)}, f32[256,768]{1,0:T(8,128)}, f32[192,768]{1,0:T(8,128)}, f32[192,768]{1,0:T(8,128)}, f32[6,2304]{1,0:T(8,128)}, /*index=5...) custom-call(bf16[256,768]{1,0:T(8,128)(2,1)} %x_hbm.1, f32[256,768]{1,0:T(8,128)} %cot_hbm.1, s32[2,128]{1,0:T(2,128)} %bitcast.16, ...), custom_call_target="tpu_custom_call" | custom-call | tf_op jit(solution)/shard_map/layer/pallas_call | solution.py:1124
  148.2 2.8 %hand_over.1 = (f32[256,768]{1,0:T(8,128)}, f32[256,768]{1,0:T(8,128)}, f32[192,768]{1,0:T(8,128)}, f32[192,768]{1,0:T(8,128)}, f32[6,2304]{1,0:T(8,128)}, /*index=5*/f32[6,768]{1,0:T(8,128)}, f32[6,8]{1,0:T(8,128)}) custom-call(f32[256,768]{1,0:T(8,128)} %get-tuple-element.25.refs_0_, f32[256,768]{1,0:T(8,128)} %get-tuple-element.26.refs_1_, ...), custom_call_target="tpu_custom_call" | custom-call | tf_op jit(solution)/shard_map/hand_over/pallas_call | solution.py:1246
  151.0 0.0 copy-start
  151.0 0.6 copy-done
  151.6 0.6 slice_bitcast_fusion
  152.2 0.6 slice_bitcast_fusion.1
  (3 shorter events, 0.0 us)
Async XLA Ops:
  0.7 0.7 copy-start.1
  0.7 0.7 copy-start.2
  0.7 0.7 copy-start.3
  151.0 0.6 copy-start

commit v4 on v3

--- a/solution.py
+++ b/solution.py
@@ -217,7 +217,6 @@
         self.w, self.axis, self.place, self.rows, self.half = w, axis, place, rows, rows // 2
         self.relayed, self.landed = relayed, landed
         self.send, self.recv, self.base = send, recv, base
-        self.step = min(32, self.half)
         self.copies = {}
 
     def _go(self, k, src, dst, step):
@@ -245,17 +244,17 @@
     def relay(self):
         self.copies[0].wait_recv()
         low = self._part(self.place(1), 0)
-        add_rows(self.half, self.step, low, low, self.relayed.at[0])
+        add_rows(self.half, 32, low, low, self.relayed.at[0])
         self._go(4, low, self._part(self.landed.at[0], 0), 1)
         self.copies[1].wait_recv()
         high = self._part(self.place(-1), 1)
-        add_rows(self.half, self.step, high, high, self.relayed.at[1])
+        add_rows(self.half, 32, high, high, self.relayed.at[1])
         self._go(5, high, self._part(self.landed.at[1], 1), -1)
 
     def finish(self, dst):
         for k in (2, 3, 4, 5):
             self.copies[k].wait_recv()
-        add_rows(self.rows, self.step, dst, self.place(0), self.landed.at[0], self.landed.at[1])
+        add_rows(self.rows, 32, dst, self.place(0), self.landed.at[0], self.landed.at[1])
 
     def drain(self):
         for k in range(6):
@@ -310,7 +309,9 @@
     grad_qkv_ref,
     grad_attn_ref,
     router_out_ref,
-    extra_out_ref,
+    gain_one_ref,
+    gain_two_ref,
+    bias_ref,
     x_ref,
     cot_ref,
     ids_ref,
@@ -357,18 +358,10 @@
     relayed,
     landed,
     ddense,
-    dthird,
     crossed,
-    crossed_third,
     x_relayed,
     x_landed,
     dp_got,
-    third_relayed,
-    third_landed,
-    third_relayed_y,
-    third_landed_y,
-    third_sum,
-    third_last,
     dp_extra,
     extra_mine,
     extra_sum,
@@ -403,8 +396,6 @@
     sdp_recv,
     sa_send,
     sa_recv,
-    st_send,
-    st_recv,
 ):
     w = Where()
     scale = HEAD_DIM ** (-0.5)
@@ -580,8 +571,10 @@
     for n in range(2):
         one[n].finish()
         two[n, 2].start()
-    ring.finish()
-    pair.append(across(3, dense.at[w.at("x", 2)]))
+    for k in range(2):
+        ring.copies[4 + k].wait_recv()
+        half = pl.ds(k * (WIDTH // 2), WIDTH // 2)
+        pair.append(across(3 + k, dense.at[w.at("x", 2), half]))
     for copy in pair:
         copy.wait_recv()
     for e in range(6):
@@ -842,25 +835,21 @@
     second_norm_back(0)
     attention_back(0, 0, 3)
 
-    third = 2 * COLS // 3
-
-    def dense_block(e, value):
-        value = value.astype(BF16)
-        ddense[e] = value[:, :third]
-        dthird[e % 2, :, e // 2] = value[:, third:].reshape(DP, ROWS, COLS - third)
-
-    for e in range(6):
-        dense_block(e, contract_first(n1[...], dqkv[:, e * COLS : (e + 1) * COLS]))
-    for e in range(2):
-        dense_block(6 + e, contract_first(attn[...], da[:, e * COLS : (e + 1) * COLS]))
-
-    pair_third = remote(
-        dthird.at[1 - w.c], crossed_third, sx_send.at[10], sx_recv.at[10], w.partner
-    )
-    pair_third.start()
+    def dense_gradient(e):
+        @pl.when(e < 6)
+        def _():
+            columns = pl.ds(pl.multiple_of(e * COLS, 128), COLS)
+            ddense[e] = contract_first(n1[...], dqkv[:, columns]).astype(BF16)
+
+        @pl.when(e >= 6)
+        def _():
+            columns = pl.ds(pl.multiple_of((e - 6) * COLS, 128), COLS)
+            ddense[e] = contract_first(attn[...], da[:, columns]).astype(BF16)
+
     pair_sum = []
     for k, o in enumerate(order):
         to = lax.rem(w.x + o + 4, 4)
+        dense_gradient(2 * to + 1 - w.c)
         copy = remote(
             ddense.at[2 * to + 1 - w.c],
             crossed.at[to],
@@ -870,27 +859,7 @@
         )
         copy.start()
         pair_sum.append(copy)
-
-    def third_rows(s):
-        return dthird.at[w.c, pl.ds(4 * lax.rem(w.z + s + 4, 4), 4)]
-
-    zsum = RingSum(w, "z", third_rows, 4, third_relayed, third_landed, st_send, st_recv, 3)
-    ysum = RingSum(
-        w,
-        "y",
-        lambda s: dthird.at[w.c, w.at("y", s)],
-        4,
-        third_relayed_y,
-        third_landed_y,
-        st_send,
-        st_recv,
-        9,
-    )
-
-    def add_third(k, n):
-        total = dthird[w.c, k].astype(F32) + crossed_third[k].astype(F32)
-        dthird[w.c, k] = total.astype(BF16)
-        return n
+        dense_gradient(2 * to + w.c)
 
     def add_pair(k):
         pair_sum[k].wait_recv()
@@ -898,10 +867,6 @@
         here = ddense.at[2 * to + w.c]
         add_rows(WIDTH, 32, here, here, crossed.at[to])
 
-    pair_third.wait_recv()
-    lax.fori_loop(0, DP, add_third, 0)
-    zsum.far()
-    zsum.near()
     xsum = RingSum(
         w, "x", lambda s: ddense.at[w.at("x", s)], WIDTH, x_relayed, x_landed, sx_send, sx_recv, 0
     )
@@ -924,17 +889,13 @@
         u1 - r1 * jnp.mean(u1 * r1, axis=-1, keepdims=True)
     )
     store(grad_tokens_ref, grad_tokens_hbm)
-    zsum.relay()
-    for n in range(2):
-        sum2[n, 2].finish(grads.at[n, w.at2(axes[n][0], 2, 0)])
-        sum1[n].far()
-
     def bucket(b, n):
         hit = (buckets_ref[...] == b)[None]
         bias_rows[b] = jnp.sum(jnp.where(hit, ds_sum[...], 0.0), axis=1)
         return n
 
     lax.fori_loop(0, BUCKETS, bucket, 0)
+    xsum.relay()
     per_bucket = jnp.sum(bias_rows[...], axis=2)
     per_bucket = jnp.concatenate([per_bucket, jnp.zeros((BUCKETS, 4), F32)], axis=1)
     owner_f = owner_ref[...].astype(F32)
@@ -978,32 +939,13 @@
 
     lax.fori_loop(1, DP, start_extra, 0)
     dp_extra[w.dp] = extra_mine[w.dp]
-    zsum.finish(third_rows(0))
-    ysum.far()
-    ysum.near()
-    xsum.relay()
+    for n in range(2):
+        sum2[n, 2].finish(grads.at[n, w.at2(axes[n][0], 2, 0)])
+        sum1[n].far()
     for n in range(2):
         for o in (1, -1):
             sum2[n, o].finish(grads.at[n, w.at2(axes[n][0], o, 0)])
         sum1[n].near()
-    for n in range(2):
-        sum1[n].relay()
-    for n in range(2):
-        sum2[n, 0].finish(grads.at[n, w.dp])
-    ysum.relay()
-    ysum.finish(third_sum)
-    third_x = []
-    for k, o in enumerate((2, 1, -1)):
-        copy = remote(
-            third_sum.at[lax.rem(w.x + o + 4, 4)],
-            third_last.at[w.x],
-            st_send.at[k],
-            st_recv.at[k],
-            w.dev("x", o),
-        )
-        copy.start()
-        third_x.append(copy)
-    third_last[w.x] = third_sum[w.x]
     xsum.finish(ddense.at[w.e])
 
     def rows_of(dp):
@@ -1031,14 +973,10 @@
 
     lax.fori_loop(1, DP, start_dense, 0)
     dp_got[w.dp] = ddense[w.e, rows_of(w.dp)]
-    for n, (ref, hbm) in enumerate(((in_ref, in_hbm), (out_ref, out_hbm))):
-        sum1[n].finish(ref)
-        store(ref, hbm)
-    for copy in third_x:
-        copy.wait_recv()
-    last_third = third_last[0].astype(F32)
-    for k in range(1, 4):
-        last_third = last_third + third_last[k].astype(F32)
+    for n in range(2):
+        sum1[n].relay()
+    for n in range(2):
+        sum2[n, 0].finish(grads.at[n, w.dp])
     lax.fori_loop(1, DP, end_dense, 0)
     total = dp_got[0].astype(F32)
     extra_total = dp_extra[0]
@@ -1046,7 +984,7 @@
         total = total + dp_got[k].astype(F32)
         extra_total = extra_total + dp_extra[k]
     extra_sum[...] = extra_total
-    flat = jnp.concatenate([total[:, :128], total[:, 128:], last_third], axis=0)
+    flat = jnp.concatenate([total[:, c * 128 : (c + 1) * 128] for c in range(3)], axis=0)
     last[...] = (
         jnp.dot(spread_ref[...], flat.astype(BF16), preferred_element_type=F32)
         .astype(BF16)
@@ -1075,19 +1013,23 @@
     lax.fori_loop(1, EXPERTS, start_owner, 0)
     last_got[w.e] = last[w.e]
     extra_got[w.e] = extra_sum[...]
+    for n, (ref, hbm) in enumerate(((in_ref, in_hbm), (out_ref, out_hbm))):
+        sum1[n].finish(ref)
+        store(ref, hbm)
     lax.fori_loop(1, EXPERTS, end_owner, 0)
     for e in range(EXPERTS):
         columns = last_got[e].astype(F32)
+        ref, at = (grad_qkv_ref, e * COLS) if e < 6 else (grad_attn_ref, (e - 6) * COLS)
         for c in range(3):
-            ref = grad_qkv_ref if e < 6 else grad_attn_ref
-            at = (e % 6 if e < 6 else e - 6) * COLS + c * 128
-            ref[:, at : at + 128] = columns[c * 6 : c * 6 + 6]
+            ref[:, at + c * 128 : at + (c + 1) * 128] = columns[c * 6 : c * 6 + 6]
     extra_total = extra_got[0]
     for k in range(1, EXPERTS):
         extra_total = extra_total + extra_got[k]
     extra_sum[...] = extra_total
     row = extra_sum[pl.ds(w.e, 1)]
-    extra_out_ref[...] = row
+    gain_one_ref[...] = row[:, 48:54]
+    gain_two_ref[...] = row[:, 56:62]
+    bias_ref[...] = row[:, 64:67]
     for r in range(6):
         router_out_ref[r : r + 1] = row[:, r * EXPERTS : (r + 1) * EXPERTS]
 
@@ -1098,11 +1040,9 @@
         one[n].drain()
         for o in (0, -1, 1, 2):
             two[n, o].drain()
-    for copy in (*pair_sum, pair_third, *third_x):
+    for copy in pair_sum:
         copy.wait_send()
     xsum.drain()
-    zsum.drain()
-    ysum.drain()
     for copy in stores:
         copy.wait()
     for n in range(2):
@@ -1115,7 +1055,7 @@
     hbm = pl.BlockSpec(memory_space=pl.ANY)
     vmem = pl.BlockSpec(memory_space=pltpu.VMEM)
     tokens = x.shape[0]
-    half, main = SHARD // 2, COLS - 128
+    half, main = SHARD // 2, COLS
     small = tuple(jnp.asarray(m, BF16) for m in (place_matrix(), spread_matrix(), *small_matrices()))
 
     def dma(*shape):
@@ -1131,10 +1071,12 @@
             jax.ShapeDtypeStruct((6, 3 * WIDTH), F32),
             jax.ShapeDtypeStruct((6, WIDTH), F32),
             jax.ShapeDtypeStruct((6, EXPERTS), F32),
-            jax.ShapeDtypeStruct((1, 128), F32),
+            jax.ShapeDtypeStruct((1, 6), F32),
+            jax.ShapeDtypeStruct((1, 6), F32),
+            jax.ShapeDtypeStruct((1, 3), F32),
         ),
         in_specs=[hbm] * 5 + [vmem] * 4 + [hbm] * 10,
-        out_specs=(hbm,) * 4 + (vmem,) * 4,
+        out_specs=(hbm,) * 4 + (vmem,) * 6,
         scratch_shapes=[
             *(pltpu.VMEM(a.shape, a.dtype) for a in (x, cot, ids, slots, buckets)),
             pltpu.VMEM((EXPERTS, ROWS, 128), F32),
@@ -1171,18 +1113,10 @@
             pltpu.VMEM((10, 2, half, WIDTH), BF16),
             pltpu.VMEM((10, 2, SHARD, WIDTH), BF16),
             pltpu.VMEM((EXPERTS, WIDTH, main), BF16),
-            pltpu.VMEM((2, DP, 4, ROWS, 128), BF16),
             pltpu.VMEM((4, WIDTH, main), BF16),
-            pltpu.VMEM((DP, 4, ROWS, 128), BF16),
             pltpu.VMEM((2, WIDTH // 2, main), BF16),
             pltpu.VMEM((2, WIDTH, main), BF16),
             pltpu.VMEM((DP, ROWS, main), BF16),
-            pltpu.VMEM((2, 2, 4, ROWS, 128), BF16),
-            pltpu.VMEM((2, 4, 4, ROWS, 128), BF16),
-            pltpu.VMEM((2, 2, ROWS, 128), BF16),
-            pltpu.VMEM((2, 4, ROWS, 128), BF16),
-            pltpu.VMEM((4, ROWS, 128), BF16),
-            pltpu.VMEM((4, ROWS, 128), BF16),
             pltpu.VMEM((DP, 8, 128), F32),
             pltpu.VMEM((DP, 8, 128), F32),
             pltpu.VMEM((8, 128), F32),
@@ -1205,8 +1139,8 @@
             dma(2, DP),
             dma(40),
             dma(40),
-            dma(10),
-            dma(10),
+            dma(11),
+            dma(11),
             dma(32),
             dma(32),
             dma(60),
@@ -1217,8 +1151,6 @@
             dma(2, DP),
             dma(2, EXPERTS),
             dma(2, EXPERTS),
-            dma(15),
-            dma(15),
         ],
         compiler_params=pltpu.CompilerParams(
             collective_id=0, has_side_effects=True, vmem_limit_bytes=63 * MIB
@@ -1289,19 +1221,18 @@
         w_in[0],
         w_out[0],
     )
-    output, grad_tokens, grad_in, grad_out, grad_qkv, grad_attn, grad_router = hand_over(
-        *results[:7]
-    )
-    small = results[7][0]
+    results = hand_over(*results)
+    output, grad_tokens, grad_in, grad_out, grad_qkv, grad_attn, grad_router = results[:7]
+    grad_gain_one, grad_gain_two, grad_bias = (small[0] for small in results[7:])
     return (
         output,
         grad_tokens,
         grad_qkv,
         grad_attn,
         grad_router,
-        small[48:54],
-        small[56:62],
-        small[64:67],
+        grad_gain_one,
+        grad_gain_two,
+        grad_bias,
         grad_in[None],
         grad_out[None],
     )

time: 153 us -> 146 us (0.954)
  Pallas kernels: 149 us -> 144 us
  local copies, waits for them, and re-layouts: 3.04 us -> 1.27 us
    pallas_call x1, Pallas kernels: 146 us -> 141 us  [layer(): pl.pallas_call(layer_kernel, out_shape=(jax.ShapeDtypeStruct((tokens, WID...]
where the time goes in v4:
time: 146 us
  Pallas kernels  144 us (99%)
    pallas_call x1, Pallas kernels, layer(): pl.pallas_call(layer_kernel, out_shape=(jax.ShapeDtypeStruct((tokens, WID...  141 us

profile of v4, /device:TPU:1, one launch (start us, length us, event | category | flops | bytes accessed | tf_op | source)
XLA Modules:
  0.0 146.3 jit_solution(12912421966972122967)
XLA Ops:
  0.7 0.0 copy-start
  0.7 0.0 copy-start.1
  0.7 0.0 copy-start.2
  0.7 0.6 copy-done
  1.3 0.0 copy-done.1
  1.3 0.0 copy-done.2
  1.4 0.6 concatenate.3
  2.0 141.3 %layer.1 = (f32[256,768]{1,0:T(8,128)}, f32[256,768]{1,0:T(8,128)}, f32[192,768]{1,0:T(8,128)}, f32[192,768]{1,0:T(8,128)}, f32[6,2304]{1,0:T(8,128)}, /*index=5...) custom-call(bf16[256,768]{1,0:T(8,128)(2,1)} %x_hbm.1, ...), custom_call_target="tpu_custom_call" | custom-call | tf_op jit(solution)/shard_map/layer/pallas_call | solution.py:1064
  143.2 2.9 %hand_over.1 = (f32[256,768]{1,0:T(8,128)}, f32[256,768]{1,0:T(8,128)}, f32[192,768]{1,0:T(8,128)}, f32[192,768]{1,0:T(8,128)}, f32[6,2304]{1,0:T(8,128)}, /*ind...) custom-call(f32[256,768]{1,0:T(8,128)} %get-tuple-element.30.refs_0_, ...), custom_call_target="tpu_custom_call" | custom-call | tf_op jit(solution)/shard_map/hand_over/pallas_call | solution.py:1178
  (3 shorter events, 0.0 us)
Async XLA Ops:
  0.7 0.7 copy-start
  0.7 0.7 copy-start.1
  0.7 0.7 copy-start.2
